TPU v7x, 1024 devices: a whole 4x8x16 slice. The times are simulated.
1024 devices in a mesh: outer: 64 (over x, z), inner: 16 (over y, core).
Axes of the slice: x: 4, y: 8, z: 16, core: 2. Of those that a mesh axis runs over, the one named last changes fastest.
Arguments:
- hidden_in: bfloat16 [131072, 896], P(('outer', 'inner')), may hold values from -6 to 6
- doc_ids: int32 [1024, 128], P(('outer', 'inner')), may hold values from 0 to 7, never falling along the last dimension, each value on 1 to 32 neighbouring positions
- grad_mixed: bfloat16 [131072, 896], P(('outer', 'inner')), may hold values from -6 to 6
- in_codes: bfloat16 [896, 576], P('inner'), may hold values from -1.8708287 to 1.8708287
- in_scales: float32 [28, 9], replicated, may hold values from 0.5 to 2
- out_codes: bfloat16 [448, 896], P(None, 'inner'), may hold values from -0.25 to 0.25
- out_scales: float32 [7, 28], replicated, may hold values from 0.5 to 2
Outputs:
- mixed: bfloat16 [131072, 896], P(('outer', 'inner'))
- grad_hidden: bfloat16 [131072, 896], P(('outer', 'inner'))
- grad_in_weight: float32 [516096], P(('outer', 'inner'))
- grad_out_weight: float32 [401408], P(('outer', 'inner'))
All inputs are finite; a program needn't handle non-finite values.
Results may differ from a plain program's by a relative error of at most 0.015.
Values may be sent and summed in bfloat16 or wider, within the bound.
A program may use at most 32 MiB of HBM per device.

v0:
```python
import jax
import jax.numpy as jnp
from jax import lax
from jax.sharding import PartitionSpec as P

HEAD_SIZE = 64
QUERY_HEADS = 7
KEY_VALUE_HEADS = 1
SB = 32
QUERY_COLUMNS = 448
KEY_COLUMNS = 64


rope_base = 1000000.0
norm_eps = 1e-06


def expand_scales(scales, row_block, col_block):
    return jnp.repeat(jnp.repeat(scales, row_block, axis=0), col_block, axis=1)


def rope_tables(row_docs):
    sequence_length = row_docs.shape[0]
    token_index = jnp.arange(sequence_length, dtype=jnp.int32)
    starting = jnp.concatenate([jnp.ones((1,), jnp.bool_), row_docs[1:] != row_docs[:-1]])
    doc_first = lax.cummax(jnp.where(starting, token_index, 0), axis=0)
    positions = (token_index - doc_first).astype(jnp.float32)
    half_width = HEAD_SIZE // 2
    frequency = rope_base ** (-jnp.arange(half_width, dtype=jnp.float32) * 2.0 / HEAD_SIZE)
    angles = positions[:, None] * frequency[None, :]
    return (jnp.cos(angles), jnp.sin(angles))


def apply_rotary(vectors, cosine_table, sines_lookup, direction):
    half_width = HEAD_SIZE // 2
    first_half = vectors[..., :half_width]
    second_half = vectors[..., half_width:]
    cos_b = cosine_table[:, None, :]
    sin_b = sines_lookup[:, None, :]
    return jnp.concatenate(
        [
            first_half * cos_b - direction * second_half * sin_b,
            second_half * cos_b + direction * first_half * sin_b,
        ],
        axis=-1,
    )


def attend(projected_rows, row_docs):
    sequence_length = projected_rows.shape[0]
    query_group = QUERY_HEADS // KEY_VALUE_HEADS
    cosine_table, sines_lookup = rope_tables(row_docs)
    query_rows = apply_rotary(
        projected_rows[:, :QUERY_COLUMNS].reshape(sequence_length, QUERY_HEADS, HEAD_SIZE),
        cosine_table,
        sines_lookup,
        1.0,
    )
    query_rows_batch = query_rows.astype(jnp.bfloat16).reshape(
        sequence_length, KEY_VALUE_HEADS, query_group, HEAD_SIZE
    )
    key_rows_batch = apply_rotary(
        projected_rows[:, QUERY_COLUMNS : QUERY_COLUMNS + KEY_COLUMNS].reshape(
            sequence_length, KEY_VALUE_HEADS, HEAD_SIZE
        ),
        cosine_table,
        sines_lookup,
        1.0,
    ).astype(jnp.bfloat16)
    value_rows_batch = (
        projected_rows[:, QUERY_COLUMNS + KEY_COLUMNS :]
        .reshape(sequence_length, KEY_VALUE_HEADS, HEAD_SIZE)
        .astype(jnp.bfloat16)
    )
    scores = jnp.einsum(
        "tkgd,skd->kgts", query_rows_batch, key_rows_batch, preferred_element_type=jnp.float32
    ) * HEAD_SIZE ** (-0.5)
    token_index = jnp.arange(sequence_length, dtype=jnp.int32)
    allowed = (row_docs[:, None] == row_docs[None, :]) & (
        token_index[None, :] <= token_index[:, None]
    )
    scores = jnp.where(allowed[None, None], scores, -jnp.inf)
    peak = jnp.max(scores, axis=-1, keepdims=True)
    expon = jnp.exp(scores - peak)
    probs = expon / jnp.sum(expon, axis=-1, keepdims=True)
    probs_b = probs.astype(jnp.bfloat16)
    attention_output = jnp.einsum(
        "kgts,skd->tkgd", probs_b, value_rows_batch, preferred_element_type=jnp.float32
    )
    attention_output = attention_output.reshape(sequence_length, QUERY_COLUMNS).astype(jnp.bfloat16)
    return (
        attention_output,
        (
            query_rows_batch,
            key_rows_batch,
            value_rows_batch,
            probs,
            probs_b,
            cosine_table,
            sines_lookup,
        ),
    )


def attend_back(attention_output_gradient, attention_output, saved):
    (
        query_rows_batch,
        key_rows_batch,
        value_rows_batch,
        probs,
        probs_b,
        cosine_table,
        sines_lookup,
    ) = saved
    sequence_length = attention_output.shape[0]
    query_group = QUERY_HEADS // KEY_VALUE_HEADS
    head_gradients = attention_output_gradient.reshape(
        sequence_length, KEY_VALUE_HEADS, query_group, HEAD_SIZE
    )
    attention_heads = attention_output.reshape(
        sequence_length, KEY_VALUE_HEADS, query_group, HEAD_SIZE
    )
    grad_probs = jnp.einsum(
        "tkgd,skd->kgts", head_gradients, value_rows_batch, preferred_element_type=jnp.float32
    )
    delta = jnp.einsum(
        "tkgd,tkgd->kgt", head_gradients, attention_heads, preferred_element_type=jnp.float32
    )
    grad_scores = (probs * (grad_probs - delta[..., None]) * HEAD_SIZE ** (-0.5)).astype(
        jnp.bfloat16
    )
    grad_query = jnp.einsum(
        "kgts,skd->tkgd", grad_scores, key_rows_batch, preferred_element_type=jnp.float32
    )
    grad_keys = jnp.einsum(
        "kgts,tkgd->skd", grad_scores, query_rows_batch, preferred_element_type=jnp.float32
    )
    grad_values = jnp.einsum(
        "kgts,tkgd->skd", probs_b, head_gradients, preferred_element_type=jnp.float32
    )
    grad_query = apply_rotary(
        grad_query.reshape(sequence_length, QUERY_HEADS, HEAD_SIZE),
        cosine_table,
        sines_lookup,
        -1.0,
    ).reshape(sequence_length, QUERY_COLUMNS)
    grad_keys = apply_rotary(grad_keys, cosine_table, sines_lookup, -1.0).reshape(
        sequence_length, KEY_COLUMNS
    )
    joined = jnp.concatenate(
        [grad_query, grad_keys, grad_values.reshape(sequence_length, KEY_COLUMNS)], axis=1
    )
    return joined.astype(jnp.bfloat16)


def body(hidden_in, doc_ids, grad_mixed, in_codes, in_scales, out_codes, out_scales):
    in_full = expand_scales(in_scales, SB, HEAD_SIZE)
    out_full = expand_scales(out_scales, HEAD_SIZE, SB)
    sequence_length = hidden_in.shape[0]
    rows_f = hidden_in.astype(jnp.float32)
    inverse_rms = lax.rsqrt(jnp.mean(rows_f * rows_f, axis=-1, keepdims=True) + norm_eps)
    normed = rows_f * inverse_rms
    normed_b = normed.astype(jnp.bfloat16)
    whole_in, whole_out = (
        lax.all_gather(in_codes, "inner", axis=0, tiled=True),
        lax.all_gather(out_codes, "inner", axis=1, tiled=True),
    )
    w_in = (whole_in.astype(jnp.float32) * in_full).astype(jnp.bfloat16)
    w_out = (whole_out.astype(jnp.float32) * out_full).astype(jnp.bfloat16)
    projected_rows = jnp.dot(normed_b, w_in, preferred_element_type=jnp.float32)
    attention_output, saved = attend(projected_rows, doc_ids[0])
    branch_out = jnp.dot(attention_output, w_out, preferred_element_type=jnp.float32)
    attention_output_gradient = jnp.dot(
        grad_mixed, w_out.T, preferred_element_type=jnp.float32
    ).astype(jnp.bfloat16)
    mixed = (rows_f + branch_out).astype(jnp.bfloat16)
    grad_projected = attend_back(attention_output_gradient, attention_output, saved)
    grad_normed = jnp.dot(grad_projected, w_in.T, preferred_element_type=jnp.float32)
    inner_mean = jnp.mean(grad_normed * normed, axis=-1, keepdims=True)
    grad_hidden = (
        (grad_normed - normed * inner_mean) * inverse_rms + grad_mixed.astype(jnp.float32)
    ).astype(jnp.bfloat16)
    outer_count = lax.axis_size("outer")
    inner_count = lax.axis_size("inner")
    grad_scale = (sequence_length * outer_count * inner_count) ** (-0.5)
    part_in = (
        (jnp.dot(normed_b.T, grad_projected, preferred_element_type=jnp.float32) * grad_scale)
        .astype(jnp.bfloat16)
        .reshape(-1)
    )
    part_out = (
        (jnp.dot(attention_output.T, grad_mixed, preferred_element_type=jnp.float32) * grad_scale)
        .astype(jnp.bfloat16)
        .reshape(-1)
    )
    first_in, first_out = (
        lax.all_to_all(
            part_in.reshape(outer_count, inner_count, -1),
            "inner",
            split_axis=1,
            concat_axis=1,
            tiled=True,
        ),
        lax.all_to_all(
            part_out.reshape(outer_count, inner_count, -1),
            "inner",
            split_axis=1,
            concat_axis=1,
            tiled=True,
        ),
    )
    middle_in = jnp.sum(first_in.astype(jnp.float32), axis=1)
    middle_out = jnp.sum(first_out.astype(jnp.float32), axis=1)
    second_in, second_out = (
        lax.all_to_all(
            middle_in.astype(jnp.bfloat16), "outer", split_axis=0, concat_axis=0, tiled=True
        ).astype(middle_in.dtype),
        lax.all_to_all(
            middle_out.astype(jnp.bfloat16), "outer", split_axis=0, concat_axis=0, tiled=True
        ).astype(middle_out.dtype),
    )
    grad_in_weight = jnp.sum(second_in, axis=0)
    grad_out_weight = jnp.sum(second_out, axis=0)
    return (mixed, grad_hidden, grad_in_weight, grad_out_weight)


def solution(mesh):
    in_specs = (
        P(("outer", "inner"), None),
        P(("outer", "inner"), None),
        P(("outer", "inner"), None),
        P("inner", None),
        P(),
        P(None, "inner"),
        P(),
    )
    out_specs = (
        P(("outer", "inner"), None),
        P(("outer", "inner"), None),
        P(("outer", "inner")),
        P(("outer", "inner")),
    )
    return jax.shard_map(body, mesh=mesh, in_specs=in_specs, out_specs=out_specs, check_vma=False)
```

profile of v0, /device:TPU:1, one launch (start us, length us, event | category | flops | bytes accessed | tf_op | source)
XLA Modules:
  0.0 177.4 jit_solution(13584955780588309755)
XLA Ops:
  0.7 1.1 fusion.20
  1.7 0.8 broadcast_in_dim.24
  2.7 32.5 %all_gather.6 = bf16[896,576]{1,0:T(8,128)(2,1)S(1)} all-gather(bf16[56,576]{1,0:T(8,128)(2,1)} %param.10), channel_id=1, replica_groups=mesh['outer'=64,'inner'=16] {'inner'}, dimensions={0}, use_global_device_ids=true | all-gather | bytes 1096704 | tf_op jit(solution)/shard_map/all_gather | solution.py:165
  35.2 1.1 copy.36
  36.3 0.2 fusion
  36.5 0.7 copy-done
  37.2 0.5 fusion.28
  38.8 17.8 %all_gather.7 = bf16[448,896]{0,1:T(8,128)(2,1)S(1)} all-gather(bf16[448,56]{0,1:T(8,128)(2,1)S(1)} %copy-done.19), channel_id=1, replica_groups=mesh['outer'=64,'inner'=16] {'inner'}, dimensions={1}, use_global_device_ids=true | all-gather | bytes 852992 | tf_op jit(solution)/shard_map/all_gather | solution.py:166
  56.6 0.7 broadcast_multiply_fusion
  57.5 0.3 fusion.58
  57.9 0.7 copy-done.1
  58.7 0.2 fusion.1
  58.9 0.6 copy-done.3
  59.5 0.4 convolution_convert_fusion
  60.0 0.8 fusion.23
  60.8 0.6 copy-done.7
  61.4 1.3 multiply_convert_fusion.1
  62.6 3.6 %reshape_reshape.7 = bf16[64,16,392]{2,1,0:T(8,128)(2,1)S(1)} reshape(bf16[448,896]{1,0:T(8,128)(2,1)} %multiply_convert_fusion.1) | data formatting | bytes 1605632 | tf_op jit(solution)/shard_map/reshape;reshape | solution.py:205
  66.2 1.6 copy.46
  67.9 4.4 %all-to-all-start.2 = ((bf16[64,16,392]{2,0,1:T(8,128)(2,1)}), bf16[64,16,392]{2,0,1:T(8,128)(2,1)}, u32[]{:S(2)}, u32[]{:S(2)}) async-start(bf16[64,16,392]{2,0,1:T(8,128)(2,1)} %copy.46), calls=%async_computation.2 | async-start | bytes 2097152 | tf_op jit(solution)/shard_map/all_to_all | solution.py:204
  72.3 1.0 fusion.9
  73.4 0.2 convolution_bitcast_fusion.3
  73.8 0.2 convolution_bitcast_fusion.1
  74.0 0.3 copy-done.5
  74.3 0.2 fusion.11
  74.5 0.4 copy-done.8
  75.1 1.5 multiply_convert_fusion
  76.6 2.0 %copy.43 = bf16[896,576]{1,0:T(8,128)(2,1)S(1)} copy(bf16[896,576]{0,1:T(8,128)(2,1)} %multiply_convert_fusion) | data formatting | bytes 2064384 | tf_op jit(solution)/shard_map/convert_element_type | solution.py:188
  78.6 4.1 %reshape_reshape.6 = bf16[64,16,504]{2,1,0:T(8,128)(2,1)} reshape(bf16[896,576]{1,0:T(8,128)(2,1)S(1)} %copy.43) | data formatting | bytes 2064384 | tf_op jit(solution)/shard_map/reshape;reshape | solution.py:198
  82.7 2.8 %copy.44 = bf16[64,16,504]{2,0,1:T(8,128)(2,1)} copy(bf16[64,16,504]{2,1,0:T(8,128)(2,1)} %reshape_reshape.6) | data formatting | bytes 2064384 | tf_op jit(solution)/shard_map/reshape;reshape | solution.py:198
  85.5 14.8 %all-to-all-done.2 = bf16[64,16,392]{2,0,1:T(8,128)(2,1)} async-done(((bf16[64,16,392]{2,0,1:T(8,128)(2,1)}), bf16[64,16,392]{2,0,1:T(8,128)(2,1)}, u32[]{:S(2)}, u32[]{:S(2)}) %all-to-all-start.2) | async-done | bytes 802848 | tf_op jit(solution)/shard_map/all_to_all | solution.py:204
  100.3 3.6 %all-to-all-start = ((bf16[64,16,504]{2,0,1:T(8,128)(2,1)}), bf16[64,16,504]{2,0,1:T(8,128)(2,1)S(1)}, u32[]{:S(2)}, u32[]{:S(2)}) async-start(bf16[64,16,504]{2,0,1:T(8,128)(2,1)} %copy.44), calls=%async_computation | async-start | bytes 2097152 | tf_op jit(solution)/shard_map/all_to_all | solution.py:197
  103.9 2.1 %fusion.7 = bf16[128,896]{1,0:T(8,128)(2,1)} fusion(bf16[128,448]{0,1:T(8,128)(2,1)} %bitcast.119, bf16[448,896]{0,1:T(8,128)(2,1)S(1)} %fusion.1, bf16[128,896]{1,0:T(8,128)(2,1)S(1)} %copy-done), kind=kOutput, calls=%fused_computation.14 | convolution fusion | flops 103104512 | bytes 1376256 | tf_op jit(solution)/shard_map/dot_general | solution.py:172
  106.0 0.5 fusion.15
  106.5 1.4 reduce_sum.74
  107.9 0.5 broadcast.163
  108.4 0.7 reduce.10
  109.1 0.7 reshape.376
  109.8 21.9 %all-to-all-done = bf16[64,16,504]{2,0,1:T(8,128)(2,1)S(1)} async-done(((bf16[64,16,504]{2,0,1:T(8,128)(2,1)}), bf16[64,16,504]{2,0,1:T(8,128)(2,1)S(1)}, u32[]{:S(2)}, u32[]{:S(2)}) %all-to-all-start) | async-done | bytes 1032224 | tf_op jit(solution)/shard_map/all_to_all | solution.py:197
  131.8 12.4 %all-to-all-start.3 = ((bf16[64,2,196]{2,1,0:T(2,128)(2,1)}), bf16[64,2,196]{2,1,0:T(2,128)(2,1)S(1)}, u32[]{:S(2)}, u32[]{:S(2)}) async-start(bf16[64,2,196]{2,1,0:T(2,128)(2,1)} %reshape.376), calls=%async_computation.3 | async-start | bytes 131072 | tf_op jit(solution)/shard_map/all_to_all | solution.py:218
  144.4 0.7 reduce.9
  145.1 0.7 reshape.374
  145.8 12.3 %all-to-all-done.3 = bf16[64,2,196]{2,1,0:T(2,128)(2,1)S(1)} async-done(((bf16[64,2,196]{2,1,0:T(2,128)(2,1)}), bf16[64,2,196]{2,1,0:T(2,128)(2,1)S(1)}, u32[]{:S(2)}, u32[]{:S(2)}) %all-to-all-start.3) | async-done | bytes 50208 | tf_op jit(solution)/shard_map/all_to_all | solution.py:218
  158.1 4.9 %all-to-all-start.1 = ((bf16[64,2,252]{2,1,0:T(2,128)(2,1)}), bf16[64,2,252]{2,1,0:T(2,128)(2,1)S(1)}, u32[]{:S(2)}, u32[]{:S(2)}) async-start(bf16[64,2,252]{2,1,0:T(2,128)(2,1)} %reshape.374), calls=%async_computation.1 | async-start | bytes 131072 | tf_op jit(solution)/shard_map/all_to_all | solution.py:215
  163.0 0.9 fusion.19
  164.0 0.8 convert_reduce_fusion
  164.8 11.7 %all-to-all-done.1 = bf16[64,2,252]{2,1,0:T(2,128)(2,1)S(1)} async-done(((bf16[64,2,252]{2,1,0:T(2,128)(2,1)}), bf16[64,2,252]{2,1,0:T(2,128)(2,1)S(1)}, u32[]{:S(2)}, u32[]{:S(2)}) %all-to-all-start.1) | async-done | bytes 64544 | tf_op jit(solution)/shard_map/all_to_all | solution.py:215
  176.6 0.8 convert_reduce_fusion.1
  (81 shorter events, 2.4 us)
Async XLA Ops:
  0.6 56.7 %copy-start.23 = (f32[32]{0:T(128)}, f32[32]{0:T(128)S(1)}, u32[]{:S(2)}) copy-start(f32[32]{0:T(128)S(1)} %multiply_power_fusion) | copy-start | bytes 388
  1.7 34.7 %copy-start.20 = (f32[128]{0:T(128)}, f32[128]{0:T(128)S(1)}, u32[]{:S(2)}) copy-start(f32[128]{0:T(128)S(1)} %add_rsqrt_fusion) | copy-start | bytes 1540
  36.2 0.9 copy-start
  37.2 0.7 copy-start.29
  37.2 0.7 copy-start.28
  37.2 1.6 copy-start.19
  37.7 22.3 %copy-start.6 = (f32[128,576]{0,1:T(8,128)}, f32[128,576]{0,1:T(8,128)S(1)}, u32[]{:S(2)}) copy-start(f32[128,576]{0,1:T(8,128)S(1)} %fusion.28) | copy-start | bytes 884740
  38.6 18.9 %copy-start.25 = (f32[128]{0:T(128)}, f32[128]{0:T(128)S(1)}, u32[]{:S(2)}) copy-start(f32[128]{0:T(128)S(1)} %subtract_convert_fusion.2) | copy-start | bytes 1540
  57.5 1.3 copy-start.12
  57.8 0.8 copy-start.1
  58.6 0.9 copy-start.3
  58.7 1.3 copy-start.4
  59.9 0.8 copy-start.10
  60.8 0.6 copy-start.7
  67.9 4.4 %copy-start.2 = (f32[1,7,128,128]{2,3,1,0:T(8,128)S(1)}, f32[1,7,128,128]{2,3,1,0:T(8,128)}, u32[]{:S(2)}) copy-start(f32[1,7,128,128]{2,3,1,0:T(8,128)} %copy-done.1) | copy-start | bytes 1376260
  67.9 4.4 %copy-start.11 = (bf16[448,128]{1,0:T(8,128)(2,1)S(1)}, bf16[448,128]{1,0:T(8,128)(2,1)}, u32[]{:S(2)}) copy-start(bf16[448,128]{1,0:T(8,128)(2,1)} %copy-done.10) | copy-start | bytes 344068
  67.9 4.4 %copy-start.27 = (f32[7,128]{1,0:T(8,128)S(1)}, f32[7,128]{1,0:T(8,128)}, u32[]{:S(2)}) copy-start(f32[7,128]{1,0:T(8,128)} %get-tuple-element.17) | copy-start | bytes 10756
  67.9 32.4 %all-to-all-start.2 = ((bf16[64,16,392]{2,0,1:T(8,128)(2,1)}), bf16[64,16,392]{2,0,1:T(8,128)(2,1)}, u32[]{:S(2)}, u32[]{:S(2)}) async-start(bf16[64,16,392]{2,0,1:T(8,128)(2,1)} %copy.46), calls=%async_computation.2 | async-start | bytes 2097152 | tf_op jit(solution)/shard_map/all_to_all | solution.py:204
  72.2 1.1 copy-start.13
  72.3 1.3 copy-start.24
  72.3 1.3 copy-start.26
  72.3 1.6 copy-start.18
  73.3 0.9 copy-start.5
  73.3 1.7 copy-start.21
  73.8 0.7 copy-start.16
  74.3 0.6 copy-start.8
  74.5 0.6 copy-start.14
  100.3 31.5 %all-to-all-start = ((bf16[64,16,504]{2,0,1:T(8,128)(2,1)}), bf16[64,16,504]{2,0,1:T(8,128)(2,1)S(1)}, u32[]{:S(2)}, u32[]{:S(2)}) async-start(bf16[64,16,504]{2,0,1:T(8,128)(2,1)} %copy.44), calls=%async_computation | async-start | bytes 2097152 | tf_op jit(solution)/shard_map/all_to_all | solution.py:197
  103.9 2.1 %copy-start.9 = (bf16[128,7,64]{0,2,1:T(8,128)(2,1)S(1)}, bf16[128,7,64]{0,2,1:T(8,128)(2,1)}, u32[]{:S(2)}) copy-start(bf16[128,7,64]{0,2,1:T(8,128)(2,1)} %copy-done.8) | copy-start | bytes 344068
  103.9 2.1 %copy-start.15 = (bf16[128,64]{0,1:T(8,128)(2,1)S(1)}, bf16[128,64]{0,1:T(8,128)(2,1)}, u32[]{:S(2)}) copy-start(bf16[128,64]{0,1:T(8,128)(2,1)} %copy-done.14) | copy-start | bytes 49156
  103.9 2.1 %copy-start.17 = (bf16[128,64]{0,1:T(8,128)(2,1)S(1)}, bf16[128,64]{0,1:T(8,128)(2,1)}, u32[]{:S(2)}) copy-start(bf16[128,64]{0,1:T(8,128)(2,1)} %copy-done.16) | copy-start | bytes 49156
  103.9 2.1 %copy-start.22 = (f32[128]{0:T(128)S(1)}, f32[128]{0:T(128)}, u32[]{:S(2)}) copy-start(f32[128]{0:T(128)} %copy-done.20) | copy-start | bytes 1540
  131.8 26.3 %all-to-all-start.3 = ((bf16[64,2,196]{2,1,0:T(2,128)(2,1)}), bf16[64,2,196]{2,1,0:T(2,128)(2,1)S(1)}, u32[]{:S(2)}, u32[]{:S(2)}) async-start(bf16[64,2,196]{2,1,0:T(2,128)(2,1)} %reshape.376), calls=%async_computation.3 | async-start | bytes 131072 | tf_op jit(solution)/shard_map/all_to_all | solution.py:218
  158.1 18.4 %all-to-all-start.1 = ((bf16[64,2,252]{2,1,0:T(2,128)(2,1)}), bf16[64,2,252]{2,1,0:T(2,128)(2,1)S(1)}, u32[]{:S(2)}, u32[]{:S(2)}) async-start(bf16[64,2,252]{2,1,0:T(2,128)(2,1)} %reshape.374), calls=%async_computation.1 | async-start | bytes 131072 | tf_op jit(solution)/shard_map/all_to_all | solution.py:215
where the time goes:
time: 178 us; the launch traced here: 177 us
  waiting for transfers between devices  60.8 us (34%)
  blocking collectives  50.3 us (28%)
  starting transfers between devices  25.2 us (14%)
  local copies, waits for them, and re-layouts  22.5 us (13%)
  matrix products  8.85 us (5%)
  other arithmetic  8.55 us (5%)
    all_gather x1, blocking collectives, body(): lax.all_gather(in_codes, 'inner', axis=0, tiled=True)  32.5 us
    all_to_all x1, waiting for transfers between devices, body(): lax.all_to_all(part_in.reshape(outer_count, inner_count, -1), 'inner', sp...  21.9 us
    all_gather x1, blocking collectives, body(): lax.all_gather(out_codes, 'inner', axis=1, tiled=True)  17.8 us
    all_to_all x1, waiting for transfers between devices, body(): lax.all_to_all(part_out.reshape(outer_count, inner_count, -1), 'inner', s...  14.8 us
    all_to_all x1, starting transfers between devices, body(): lax.all_to_all(middle_out.astype(jnp.bfloat16), 'outer', split_axis=0, co...  12.4 us
    all_to_all x1, waiting for transfers between devices, body(): lax.all_to_all(middle_out.astype(jnp.bfloat16), 'outer', split_axis=0, co...  12.3 us
    all_to_all x1, waiting for transfers between devices, body(): lax.all_to_all(middle_in.astype(jnp.bfloat16), 'outer', split_axis=0, con...  11.7 us
    another operation x2, local copies, waits for them, and re-layouts, body(): part_in.reshape(outer_count, inner_count, -1)  6.89 us
  transfers between devices with their start and end apart: 4, of which 4 were waited for; matrix products, arithmetic and copies ran while one was open for 12% of the time, Pallas kernels for 0%

commit v1 on v0

v1 whole, which is shorter than its diff:
```python
import math

import jax
import jax.numpy as jnp
from jax import lax
from jax.experimental import pallas as pl
from jax.experimental.pallas import tpu as pltpu
from jax.sharding import PartitionSpec as P

MESH = pl.DeviceIdType.MESH
F32, BF16 = jnp.float32, jnp.bfloat16
D, HEADS, HS = 896, 7, 64
TOK = 128
NX, NZ, NY = 4, 16, 8
ROPE_BASE = 1000000.0
EPS = 1e-06
VMEM = pltpu.VMEM
NT = (((1,), (1,)), ((), ()))
TN = (((0,), (0,)), ((), ()))


def coords():
    o = lax.axis_index("outer")
    i = lax.axis_index("inner")
    return lax.div(o, 16), lax.rem(o, 16), lax.div(i, 2), lax.rem(i, 2)


def device(x, z, y, c):
    return (x * 16 + z, y * 2 + c)


def signal(sem, dev):
    pl.semaphore_signal(sem, inc=1, device_id=dev, device_id_type=MESH)


def remote(src, dst, send, recv, dev):
    return pltpu.make_async_remote_copy(
        src_ref=src, dst_ref=dst, send_sem=send, recv_sem=recv, device_id=dev, device_id_type=MESH
    )


def lanes(shape, dim=1):
    return lax.broadcasted_iota(jnp.int32, shape, dim)


def swap_halves(v):
    low = (lanes(v.shape) & 63) < 32
    return jnp.where(low, pltpu.roll(v, 96, 1), pltpu.roll(v, 32, 1))


def allowed_pairs(doc_ref):
    row = jnp.broadcast_to(doc_ref[...].astype(F32), (TOK, TOK))
    return (row == row.T) & (lanes((TOK, TOK)) <= lanes((TOK, TOK), 0))


def gather_kernel(
    codes_ref, scale_ref, hid_ref, doc_ref,
    w_ref, nb_ref, irms_ref, cos_ref, sin_ref,
    own, ysend, yrecv, csend, crecv, lsem,
):
    x, z, y, c = coords()
    me = 2 * y + c
    sib = device(x, z, y, 1 - c)
    peers = [lax.rem(y + k, NY) for k in range(1, NY)]
    barrier = pltpu.get_barrier_semaphore()
    signal(barrier, sib)
    for p in peers:
        signal(barrier, device(x, z, p, c))

    first = lax.div(7 * me, 4)
    start = 56 * me - 32 * first
    block = (lanes((56, 1024), 0) + start) >> 5
    s0 = scale_ref[pl.ds(first, 1), :]
    s1 = scale_ref[pl.ds(first + 1, 1), :]
    s2 = scale_ref[pl.ds(jnp.minimum(first + 2, 27), 1), :]
    scale = jnp.where(block == 0, s0, jnp.where(block == 1, s1, s2))
    own[...] = (codes_ref[...].astype(F32) * scale).astype(BF16)
    local = pltpu.make_async_copy(own, w_ref.at[me], lsem)
    local.start()
    pl.semaphore_wait(barrier, NY)
    copies = []
    for k, p in enumerate(peers):
        cp = remote(own, w_ref.at[me], ysend.at[k], yrecv.at[y], device(x, z, p, c))
        cp.start()
        copies.append(cp)
    cp = remote(own, w_ref.at[me], csend.at[y], crecv.at[y], sib)
    cp.start()
    copies.append(cp)

    rows = hid_ref[...].astype(F32)
    irms = lax.rsqrt(jnp.mean(rows * rows, axis=1, keepdims=True) + EPS)
    nb_ref[...] = (rows * irms).astype(BF16)
    irms_ref[...] = jnp.broadcast_to(irms, (TOK, 128))
    pos = jnp.sum(jnp.where(allowed_pairs(doc_ref), 1.0, 0.0), axis=1, keepdims=True) - 1.0
    lane = lanes((TOK, 128))
    freq = jnp.exp((lane & 31).astype(F32) * (-2.0 * math.log(ROPE_BASE) / HS))
    angle = pos * freq
    cos_ref[...] = jnp.cos(angle)
    sine = jnp.sin(angle)
    sin_ref[...] = jnp.where((lane & 63) < 32, -sine, sine)

    for p in peers:
        slot = w_ref.at[2 * p + c]
        remote(own, slot, ysend.at[0], yrecv.at[p], sib).wait_recv()
        cp = remote(slot, slot, csend.at[p], crecv.at[p], sib)
        cp.start()
        copies.append(cp)
    for p in range(NY):
        slot = w_ref.at[2 * p + 1 - c]
        remote(own, slot, csend.at[0], crecv.at[p], sib).wait_recv()
    for cp in copies:
        cp.wait_send()
    local.wait()


def main_kernel(
    w_ref, hid_ref, gm_ref, doc_ref, nb_ref, irms_ref, cos_ref, sin_ref,
    mixed_ref, gh_ref, gout_ref,
    mixbuf, ghbuf, pin, pout, cin, cout, xin, xout, xrin, xrout, ybuf, yrbuf, msg, rbuf,
    cs, cr, xs, xr, ys, yr, fs, fr, ls,
):
    x, z, y, c = coords()
    me = 2 * y + c
    sib = device(x, z, y, 1 - c)
    xpeers = [lax.rem(x + k, NX) for k in range(1, NX)]
    ypeers = [lax.rem(y + k, NY) for k in range(1, NY)]
    owner = 8 * c + y
    diagonal = z == owner
    barrier = pltpu.get_barrier_semaphore()
    signal(barrier, sib)
    for p in xpeers:
        signal(barrier, device(p, z, y, c))
    for p in ypeers:
        signal(barrier, device(x, z, p, c))
    sy, sc = lax.rem(z, 8), lax.div(z, 8)
    for k in range(1, NZ):
        signal(barrier, device(x, lax.rem(z + k, NZ), sy, sc))

    @pl.when(jnp.logical_not(diagonal))
    def _():
        signal(barrier, device(x, z, sy, sc))

    lo = lanes((TOK, 128)) < 64
    cos, sin = cos_ref[...], sin_ref[...]
    grad_scale = 131072 ** (-0.5)
    zero = jnp.zeros((TOK, 128), F32)

    proj = jnp.dot(nb_ref[...], w_ref[:, :640], preferred_element_type=F32)
    q = []
    for t in range(4):
        v = proj[:, 128 * t : 128 * t + 128]
        q.append(v * cos + swap_halves(v) * sin)
    k_hi = jnp.where(lo, zero, q[3])
    k_lo = pltpu.roll(k_hi, 64, 1)
    q[3] = jnp.where(lo, q[3], zero)
    qb = [v.astype(BF16) for v in q]
    kk = jnp.concatenate([k_lo.astype(BF16), k_hi.astype(BF16)], axis=0)
    v_lo = jnp.where(lo, proj[:, 512:640], zero)
    v_hi = pltpu.roll(v_lo, 64, 1)
    vv = jnp.concatenate([v_lo.astype(BF16), v_hi.astype(BF16)], axis=0)
    allowed = allowed_pairs(doc_ref)
    probs, pb = [], []
    for t in range(4):
        s2 = lax.dot_general(qb[t], kk if t < 3 else kk[:128], NT, preferred_element_type=F32)
        for h in range(2 if t < 3 else 1):
            s = jnp.where(allowed, s2[:, 128 * h : 128 * h + 128] * 0.125, -1e30)
            e = jnp.exp(s - jnp.max(s, axis=1, keepdims=True))
            p = e * (1.0 / jnp.sum(e, axis=1, keepdims=True))
            probs.append(p)
            pb.append(p.astype(BF16))
    att = [jnp.dot(pb[0], vv[128:], preferred_element_type=F32).astype(BF16)]
    for t in range(1, 4):
        pair = jnp.concatenate([pb[2 * t - 1], pb[2 * t]], axis=1)
        att.append(jnp.dot(pair, vv, preferred_element_type=F32).astype(BF16))
    a = jnp.concatenate(att, axis=1)
    gm = gm_ref[...]
    part = lax.dot_general(a, gm, TN, preferred_element_type=F32)
    for h in range(2):
        for p in range(NX):
            r = 64 + 112 * p + 56 * h
            pout[h, p] = (part[r : r + 56] * grad_scale).astype(BF16)
    pl.semaphore_wait(barrier, 27 - diagonal.astype(jnp.int32))
    copies = []
    for k in range(NX):
        p = lax.rem(x + 1 + k, NX)
        cp = remote(pout.at[1 - c, p], cout.at[p], cs.at[k], cr.at[p], sib)
        cp.start()
        copies.append(cp)

    ga = jnp.dot(gm, w_ref[:, 512:], preferred_element_type=F32)
    g = [ga[:, 128 * t : 128 * t + 128] for t in range(4)]
    g[0] = jnp.where(lo, zero, g[0])
    gb = [v.astype(BF16) for v in g]
    gs = [None] * 7
    for t in range(4):
        g2 = lax.dot_general(gb[t], vv if t > 0 else vv[128:], NT, preferred_element_type=F32)
        prod = gb[t].astype(F32) * att[t].astype(F32)
        for h in range(2 if t > 0 else 1):
            head = 2 * t - 1 + h if t > 0 else 0
            if t == 0:
                delta = jnp.sum(prod, axis=1, keepdims=True)
            else:
                delta = jnp.sum(jnp.where(lo, prod, zero) if h == 0 else jnp.where(lo, zero, prod), axis=1, keepdims=True)
            gp = g2[:, 128 * h : 128 * h + 128]
            gs[head] = (probs[head] * (gp - delta) * 0.125).astype(BF16)
    zb = jnp.zeros((TOK, 128), BF16)
    q_rows = [jnp.where(lo, q[h // 2], zero).astype(BF16) if h % 2 == 0 else jnp.where(lo, zero, q[h // 2]).astype(BF16) for h in range(7)]
    g_rows = [gb[0]] + [
        (jnp.where(lo, g[(h + 1) // 2], zero) if h % 2 == 1 else jnp.where(lo, zero, g[h // 2])).astype(BF16) for h in range(1, 7)
    ]
    gk = lax.dot_general(jnp.concatenate(gs, axis=0), jnp.concatenate(q_rows, axis=0), TN, preferred_element_type=F32)
    gk = gk + pltpu.roll(gk, 64, 1)
    gv = lax.dot_general(jnp.concatenate(pb, axis=0), jnp.concatenate(g_rows, axis=0), TN, preferred_element_type=F32)
    gv = gv + pltpu.roll(gv, 64, 1)
    tiles = []
    for t in range(4):
        if t < 3:
            pair = jnp.concatenate([gs[2 * t], gs[2 * t + 1]], axis=1)
            v = jnp.dot(pair, kk, preferred_element_type=F32)
        else:
            v = jnp.dot(gs[6], kk[:128], preferred_element_type=F32)
            v = jnp.where(lo, v, gk)
        tiles.append((v * cos - swap_halves(v) * sin).astype(BF16))
    tiles.append(jnp.where(lo, gv, zero).astype(BF16))
    gpa = jnp.concatenate(tiles, axis=1)
    part = lax.dot_general(nb_ref[...], gpa, TN, preferred_element_type=F32)
    for h in range(2):
        for p in range(NX):
            r = 224 * p + 112 * h
            pin[h, p] = (part[r : r + 112] * grad_scale).astype(BF16)
    for k in range(NX):
        p = lax.rem(x + 1 + k, NX)
        cp = remote(pin.at[1 - c, p], cin.at[p], cs.at[4 + k], cr.at[4 + p], sib)
        cp.start()
        copies.append(cp)

    sum_out = sum_in = None
    for k in range(NX):
        p = lax.rem(x + 1 + k, NX)
        remote(pout.at[c, p], cout.at[p], cs.at[0], cr.at[p], sib).wait_recv()
        s = pout[c, p].astype(F32) + cout[p].astype(F32)
        if k < NX - 1:
            xout[k] = s.astype(BF16)
            cp = remote(xout.at[k], xrout.at[x], xs.at[k], xr.at[x], device(p, z, y, c))
            cp.start()
            copies.append(cp)
        else:
            sum_out = s
    for k in range(NX):
        p = lax.rem(x + 1 + k, NX)
        remote(pin.at[c, p], cin.at[p], cs.at[0], cr.at[4 + p], sib).wait_recv()
        s = pin[c, p].astype(F32) + cin[p].astype(F32)
        if k < NX - 1:
            xin[k] = s.astype(BF16)
            cp = remote(xin.at[k], xrin.at[x], xs.at[4 + k], xr.at[4 + x], device(p, z, y, c))
            cp.start()
            copies.append(cp)
        else:
            sum_in = s

    out = lax.dot_general(a, w_ref[:, 512:], NT, preferred_element_type=F32)
    mixbuf[...] = (hid_ref[...].astype(F32) + out).astype(BF16)
    mix_copy = pltpu.make_async_copy(mixbuf, mixed_ref, ls.at[0])
    mix_copy.start()
    gn = lax.dot_general(gpa, w_ref[:, :640], NT, preferred_element_type=F32)
    irms = irms_ref[:, :1]
    normed = hid_ref[...].astype(F32) * irms
    mean = jnp.mean(gn * normed, axis=1, keepdims=True)
    ghbuf[...] = ((gn - normed * mean) * irms + gm.astype(F32)).astype(BF16)
    gh_copy = pltpu.make_async_copy(ghbuf, gh_ref, ls.at[1])
    gh_copy.start()

    for p in xpeers:
        remote(xout.at[0], xrout.at[p], xs.at[0], xr.at[p], sib).wait_recv()
        sum_out = sum_out + xrout[p].astype(F32)
    high = lanes((56, 512)) >= 64
    left = jnp.where(high, pltpu.roll(sum_out[:, :512], 64, 1), 0.0)
    right = jnp.where(high, sum_out[:, 384:], 0.0)
    halves = jnp.concatenate([left, right], axis=0).astype(BF16)
    row, col = lanes((128, 112), 0), lanes((128, 112))
    j = row & 7
    q7 = 7 * ((row >> 3) & 1) + j
    pick_out = (j < 7) & (col == 7 * (row >> 4) + (q7 >> 1) + 56 * (q7 & 1))
    pick_in = (j < 7) & (col == 7 * (row >> 3) + j)
    e_out = jnp.where(pick_out, 1.0, 0.0).astype(BF16)
    e_in = jnp.where(pick_in, 1.0, 0.0).astype(BF16)
    y_out = jnp.dot(e_out, halves, preferred_element_type=F32)
    for p in xpeers:
        remote(xin.at[0], xrin.at[p], xs.at[0], xr.at[4 + p], sib).wait_recv()
        sum_in = sum_in + xrin[p].astype(F32)
    y_in = jnp.dot(e_in, sum_in.astype(BF16), preferred_element_type=F32)
    for p in range(NY):
        rows = slice(16 * p, 16 * p + 16)
        ybuf[p, :, :512] = y_in[rows, :512].astype(BF16)
        ybuf[p, :, 512:640] = (y_in[rows, 512:] + y_out[rows, :128]).astype(BF16)
        ybuf[p, :, 640:] = y_out[rows, 128:].astype(BF16)
    for k, p in enumerate(ypeers):
        cp = remote(ybuf.at[p], yrbuf.at[y], ys.at[k], yr.at[y], device(x, z, p, c))
        cp.start()
        copies.append(cp)
    total = ybuf[y].astype(F32)
    for p in ypeers:
        remote(ybuf.at[0], yrbuf.at[p], ys.at[0], yr.at[p], sib).wait_recv()
        total = total + yrbuf[p].astype(F32)

    before = pltpu.roll(total, 1, 0)
    lane = lanes((16, 1024))
    jrow = lanes((16, 1024), 0) & 7
    flat = jnp.zeros((16, 1024), F32)
    for k in range(8):
        here = jnp.where(lane < 504, pltpu.roll(total, 72 * k, 1), pltpu.roll(total, (56 * k - 72) % 1024, 1))
        past = jnp.where(lane < 504, pltpu.roll(before, (448 + 72 * k) % 1024, 1), pltpu.roll(before, (504 + 56 * k) % 1024, 1))
        old = (lane < 72 * k) | ((lane >= 504) & (lane < 504 + 56 * k))
        flat = jnp.where(jrow == k, jnp.where(old, past, here), flat)
    for t in range(8):
        msg[:, t, :] = flat[:, 128 * t : 128 * t + 128]
    for k in range(1, 16):
        i = lax.rem(me + k, 16)
        cp = remote(msg.at[i], rbuf.at[z], fs.at[k], fr.at[z], device(x, owner, lax.div(i, 2), lax.rem(i, 2)))
        cp.start()
        copies.append(cp)
    mine = remote(msg.at[me], rbuf.at[z], fs.at[0], fr.at[z], device(x, owner, y, c))
    kept = pltpu.make_async_copy(msg.at[me], rbuf.at[z], ls.at[2])

    @pl.when(diagonal)
    def _():
        kept.start()
        kept.wait()

    @pl.when(jnp.logical_not(diagonal))
    def _():
        mine.start()
        mine.wait_send()
        remote(msg.at[0], rbuf.at[z], fs.at[0], fr.at[z], sib).wait_recv()

    for k in range(1, 16):
        s = lax.rem(z + k, 16)
        remote(msg.at[0], rbuf.at[s], fs.at[0], fr.at[s], sib).wait_recv()
    gout_ref[...] = jnp.sum(rbuf[...], axis=0)
    for cp in copies:
        cp.wait_send()
    mix_copy.wait()
    gh_copy.wait()


def body(hidden_in, doc_ids, grad_mixed, in_codes, in_scales, out_codes, out_scales):
    codes = jnp.concatenate([in_codes, out_codes.T], axis=1)
    scales = jnp.repeat(jnp.concatenate([in_scales, out_scales.T], axis=1), HS, axis=1)
    vm = pl.BlockSpec(memory_space=VMEM)
    anyspace = pl.BlockSpec(memory_space=pl.ANY)
    dma = pltpu.SemaphoreType.DMA
    sds = jax.ShapeDtypeStruct
    w, nb, irms, cos, sin = pl.pallas_call(
        gather_kernel,
        out_shape=(
            sds((16, 56, 1024), BF16), sds((TOK, D), BF16), sds((TOK, 128), F32),
            sds((TOK, 128), F32), sds((TOK, 128), F32),
        ),
        in_specs=[vm] * 4,
        out_specs=(anyspace, vm, vm, vm, vm),
        scratch_shapes=[VMEM((56, 1024), BF16), dma((7,)), dma((8,)), dma((8,)), dma((8,)), dma],
        compiler_params=pltpu.CompilerParams(collective_id=0, has_side_effects=True, vmem_limit_bytes=16 << 20),
        name="gather",
    )(codes, scales, hidden_in, doc_ids)
    mixed, grad_hidden, grads = pl.pallas_call(
        main_kernel,
        out_shape=(sds((TOK, D), BF16), sds((TOK, D), BF16), sds((8, 128), F32)),
        in_specs=[vm] * 8,
        out_specs=(anyspace, anyspace, vm),
        scratch_shapes=[
            VMEM((TOK, D), BF16), VMEM((TOK, D), BF16),
            VMEM((2, 4, 112, 640), BF16), VMEM((2, 4, 56, 896), BF16),
            VMEM((4, 112, 640), BF16), VMEM((4, 56, 896), BF16),
            VMEM((3, 112, 640), BF16), VMEM((3, 56, 896), BF16),
            VMEM((4, 112, 640), BF16), VMEM((4, 56, 896), BF16),
            VMEM((8, 16, 1024), BF16), VMEM((8, 16, 1024), BF16),
            VMEM((16, 8, 128), F32), VMEM((16, 8, 128), F32),
            dma((8,)), dma((8,)), dma((8,)), dma((8,)), dma((7,)), dma((8,)), dma((16,)), dma((16,)), dma((3,)),
        ],
        compiler_params=pltpu.CompilerParams(collective_id=1, has_side_effects=True, vmem_limit_bytes=32 << 20),
        name="sublayer",
    )(w.reshape(D, 1024), hidden_in, grad_mixed, doc_ids, nb, irms, cos, sin)
    flat = grads.reshape(1024)
    return mixed, grad_hidden, flat[:504], flat[504:896]


def solution(mesh):
    rows = P(("outer", "inner"), None)
    return jax.shard_map(
        body,
        mesh=mesh,
        in_specs=(rows, rows, rows, P("inner", None), P(), P(None, "inner"), P()),
        out_specs=(rows, rows, P(("outer", "inner")), P(("outer", "inner"))),
        check_vma=False,
    )
```

time: 178 us -> 95.9 us (0.54)
  Pallas kernels: 0 us -> 84.6 us
  waiting for transfers between devices: 60.8 us -> 0 us
  blocking collectives: 50.3 us -> 0 us
  starting transfers between devices: 25.2 us -> 0 us
  local copies, waits for them, and re-layouts: 22.5 us -> 7.04 us
  matrix products: 8.85 us -> 0 us
  other arithmetic: 8.55 us -> 1.73 us
    pallas_call x0 -> x2, Pallas kernels: none -> 84.6 us  [the longest x1 50.7 us: body(): pl.pallas_call(main_kernel, out_shape=(sds((TOK, D), BF16), sds((TOK, D),...]
    all_to_all x4 -> x0, waiting for transfers between devices: 60.8 us -> none  [the longest x1 21.9 us: body(): lax.all_to_all(part_in.reshape(outer_count, inner_count, -1), 'inner', sp...]
    all_gather x2 -> x0, blocking collectives: 50.3 us -> none  [the longest x1 32.5 us: body(): lax.all_gather(in_codes, 'inner', axis=0, tiled=True)]
    all_to_all x4 -> x0, starting transfers between devices: 25.2 us -> none  [the longest x1 12.4 us: body(): lax.all_to_all(middle_out.astype(jnp.bfloat16), 'outer', split_axis=0, co...]
    another operation x4 -> x0, local copies, waits for them, and re-layouts: 12.1 us -> none  [the longest x2 6.89 us: body(): part_in.reshape(outer_count, inner_count, -1)]
    dot_general x12 -> x0, matrix products: 8.85 us -> none  [the longest x1 2.08 us: body(): jnp.dot(attention_output, w_out, preferred_element_type=jnp.float32)]
    reduce_sum x6 -> x0, other arithmetic: 4.22 us -> none  [the longest x1 1.4 us: body(): middle_out = jnp.sum(first_out.astype(jnp.float32), axis=1)]
    convert_element_type x1 -> x0, local copies, waits for them, and re-layouts: 2.02 us -> none  [body(): part_in = (jnp.dot(normed_b.T, grad_projected, preferred_element_type=jnp...]
  transfers between devices with their start and end apart: 4 -> 0, of which waited for: 4 -> 0; matrix products, arithmetic and copies ran while one was open for 12% -> 0% of each run, Pallas kernels for 0% -> 0%
where the time goes in v1:
time: 95.9 us; the launch traced here: 94 us
  Pallas kernels  84.6 us (88%)
  local copies, waits for them, and re-layouts  7.04 us (7%)
  other arithmetic  1.73 us (2%)
    pallas_call x1, Pallas kernels, body(): pl.pallas_call(main_kernel, out_shape=(sds((TOK, D), BF16), sds((TOK, D),...  50.7 us
    pallas_call x1, Pallas kernels, body(): pl.pallas_call(gather_kernel, out_shape=(sds((16, 56, 1024), BF16), sds((...  33.9 us
    unnamed x12, local copies, waits for them, and re-layouts  5.49 us

profile of v1, /device:TPU:1, one launch (start us, length us, event | category | flops | bytes accessed | tf_op | source)
XLA Modules:
  0.0 94.0 jit_solution(5596161905339810085)
XLA Ops:
  0.6 0.7 pad_maximum_fusion.1
  1.4 0.1 copy.11
  1.4 1.0 %pad_maximum_fusion.codes_ref = bf16[56,1024]{1,0:T(8,128)(2,1)S(1)} fusion(bf16[56,448]{1,0:T(8,128)(2,1)} %bitcast.7, bf16[56,576]{1,0:T(8,128)(2,1)} %param.10), kind=kLoop, calls=%fused_computation | loop fusion | flops 229376 | bytes 229376 | tf_op jit(solution)/shard_map/concatenate | solution.py:347
  2.5 0.1 broadcast_in_dim.3
  2.6 0.1 reshape.17.scale_ref
  2.7 0.0 copy-start
  2.7 0.9 copy-done
  3.6 0.0 copy-start.3
  3.6 0.7 copy-done.3
  4.3 33.9 %gather.1 = (bf16[16,56,1024]{2,1,0:T(8,128)(2,1)S(1)}, bf16[128,896]{1,0:T(8,128)(2,1)S(1)}, f32[128,128]{1,0:T(8,128)S(1)}, f32[128,128]{1,0:T(8,128)S(1)}, f32[128,128]{1,0:T(8,128)S(1)}) custom-call(bf16[56,1024]{1,0:T(8,128)(2,1)S(1)} %pad_maximum_fusion.codes_ref, f32[28,1024]{1,0:T(8,128)S(1)} %reshape.17.scale_ref, bf16[128,896]{1,0:T(8,128)(2,1)S(1)} %copy-done, ...), custom_call_target="tpu_custom_call" | custom-call | tf_op jit(solution)/shard_map/gather/pallas_call | solution.py:353
  38.2 0.0 copy-start.1
  38.2 0.9 copy-done.1
  39.1 0.0 copy-start.2
  39.1 0.9 copy-done.2
  40.0 0.0 copy-start.4
  40.0 0.7 copy-done.4
  40.7 50.7 %sublayer.1 = (bf16[128,896]{1,0:T(8,128)(2,1)S(1)}, bf16[128,896]{1,0:T(8,128)(2,1)S(1)}, f32[8,128]{1,0:T(8,128)S(1)}) custom-call(bf16[896,1024]{1,0:T(8,128)(2,1)S(1)} %bitcast.4, bf16[128,896]{1,0:T(8,128)(2,1)S(1)} %copy-done.1, bf16[128,896]{1,0:T(8,128)(2,1)S(1)} %copy-done.2, s32[1,128]{1,0:T(1,128)S(1)} %copy-done.4, ...), custom_call_target="tpu_custom_call" | custom-call | tf_op jit(solution)/shard_map/sublayer/pallas_call | solution.py:365
  91.4 0.6 slice.7
  92.1 0.6 slice.6
  92.7 0.7 copy.14
  93.4 0.7 copy.15
Async XLA Ops:
  2.7 0.9 %copy-start = (bf16[128,896]{1,0:T(8,128)(2,1)S(1)}, bf16[128,896]{1,0:T(8,128)(2,1)}, u32[]{:S(2)}) copy-start(bf16[128,896]{1,0:T(8,128)(2,1)} %hid_ref.3) | copy-start | bytes 688132
  3.6 0.7 copy-start.3
  38.2 0.9 %copy-start.1 = (bf16[128,896]{1,0:T(8,128)(2,1)S(1)}, bf16[128,896]{1,0:T(8,128)(2,1)}, u32[]{:S(2)}) copy-start(bf16[128,896]{1,0:T(8,128)(2,1)} %hid_ref.3) | copy-start | bytes 688132
  39.1 0.9 copy-start.2
  40.0 0.7 copy-start.4

commit v2 on v1

--- a/solution.py
+++ b/solution.py
@@ -54,44 +54,64 @@
 
 
 def gather_kernel(
-    codes_ref, scale_ref, hid_ref, doc_ref,
-    w_ref, nb_ref, irms_ref, cos_ref, sin_ref,
-    own, ysend, yrecv, csend, crecv, lsem,
+    inc_ref, outc_ref, ins_ref, outs_ref, hid_ref, doc_ref,
+    w_ref, nb_ref, irms_ref, cos_ref, sin_ref, mask_ref,
+    ic, oc, ins, outs, hid, doc, pad, lsem, ysend, yrecv, xsend, xrecv, csend, crecv,
 ):
     x, z, y, c = coords()
     me = 2 * y + c
     sib = device(x, z, y, 1 - c)
-    peers = [lax.rem(y + k, NY) for k in range(1, NY)]
+    xpeers = [lax.rem(x + k, NX) for k in (1, 3, 2)]
+    ypeers = [lax.rem(y + k, NY) for k in (1, 7, 2, 6, 3, 5, 4)]
     barrier = pltpu.get_barrier_semaphore()
+    for p in ypeers:
+        signal(barrier, device(x, z, p, c))
+    for p in xpeers:
+        signal(barrier, device(p, z, y, c))
     signal(barrier, sib)
-    for p in peers:
-        signal(barrier, device(x, z, p, c))
-
-    first = lax.div(7 * me, 4)
-    start = 56 * me - 32 * first
-    block = (lanes((56, 1024), 0) + start) >> 5
-    s0 = scale_ref[pl.ds(first, 1), :]
-    s1 = scale_ref[pl.ds(first + 1, 1), :]
-    s2 = scale_ref[pl.ds(jnp.minimum(first + 2, 27), 1), :]
-    scale = jnp.where(block == 0, s0, jnp.where(block == 1, s1, s2))
-    own[...] = (codes_ref[...].astype(F32) * scale).astype(BF16)
-    local = pltpu.make_async_copy(own, w_ref.at[me], lsem)
-    local.start()
-    pl.semaphore_wait(barrier, NY)
-    copies = []
-    for k, p in enumerate(peers):
-        cp = remote(own, w_ref.at[me], ysend.at[k], yrecv.at[y], device(x, z, p, c))
-        cp.start()
-        copies.append(cp)
-    cp = remote(own, w_ref.at[me], csend.at[y], crecv.at[y], sib)
-    cp.start()
-    copies.append(cp)
-
-    rows = hid_ref[...].astype(F32)
+    pairs = ((inc_ref, ic), (outc_ref, oc), (ins_ref, ins), (outs_ref, outs), (doc_ref, doc), (hid_ref, hid))
+    loads = [pltpu.make_async_copy(src, dst, lsem.at[k]) for k, (src, dst) in enumerate(pairs)]
+    for cp in loads:
+        cp.start()
+    pad[...] = jnp.zeros((56, 128), F32)
+    for cp in loads[:4]:
+        cp.wait()
+
+    shift = jnp.where(lanes((448, 512)) == lanes((448, 512), 0) + 64, 1.0, 0.0).astype(BF16)
+    turned = jnp.dot(oc[...], shift, preferred_element_type=F32)
+    block = (lanes((56, 28), 0) + 56 * me) >> 5
+    pick = jnp.where(block == lanes((56, 28)), 1.0, 0.0)
+    s_in = lax.dot_general(pick, ins[...], NT, precision=lax.Precision.HIGHEST, preferred_element_type=F32)
+    s_out = lax.dot_general(pick, outs[...], NT, precision=lax.Precision.HIGHEST, preferred_element_type=F32)
+    columns = [s_in[:, k : k + 1] for k in range(9)] + [s_out[:, k : k + 1] for k in range(7)]
+    low = lanes((56, 128)) < 64
+    pad[:, :64] = ic[:, 512:].astype(F32)
+    for t in range(8):
+        if t < 4:
+            code = ic[:, 128 * t : 128 * t + 128].astype(F32)
+        else:
+            code = turned[:, 128 * t - 512 : 128 * t - 384]
+            if t == 4:
+                code = code + pad[...]
+        scale = jnp.where(low, columns[2 * t], columns[2 * t + 1])
+        w_ref[t // 2, y, c, :, 128 * (t % 2) : 128 * (t % 2) + 128] = (code * scale).astype(BF16)
+
+    pl.semaphore_wait(barrier, 11)
+    mine = w_ref.at[x, y, c]
+    for k, p in enumerate(ypeers):
+        remote(mine, mine, ysend, yrecv.at[y], device(x, z, p, c)).start()
+    whole = w_ref.at[:, y, c]
+    remote(whole, whole, csend, crecv, sib).start()
+
+    loads[4].wait()
+    loads[5].wait()
+    rows = hid[...].astype(F32)
     irms = lax.rsqrt(jnp.mean(rows * rows, axis=1, keepdims=True) + EPS)
     nb_ref[...] = (rows * irms).astype(BF16)
     irms_ref[...] = jnp.broadcast_to(irms, (TOK, 128))
-    pos = jnp.sum(jnp.where(allowed_pairs(doc_ref), 1.0, 0.0), axis=1, keepdims=True) - 1.0
+    mask = jnp.where(allowed_pairs(doc), 1.0, 0.0)
+    mask_ref[...] = mask
+    pos = jnp.sum(mask, axis=1, keepdims=True) - 1.0
     lane = lanes((TOK, 128))
     freq = jnp.exp((lane & 31).astype(F32) * (-2.0 * math.log(ROPE_BASE) / HS))
     angle = pos * freq
@@ -99,24 +119,34 @@
     sine = jnp.sin(angle)
     sin_ref[...] = jnp.where((lane & 63) < 32, -sine, sine)
 
-    for p in peers:
-        slot = w_ref.at[2 * p + c]
-        remote(own, slot, ysend.at[0], yrecv.at[p], sib).wait_recv()
-        cp = remote(slot, slot, csend.at[p], crecv.at[p], sib)
-        cp.start()
-        copies.append(cp)
-    for p in range(NY):
-        slot = w_ref.at[2 * p + 1 - c]
-        remote(own, slot, csend.at[0], crecv.at[p], sib).wait_recv()
-    for cp in copies:
-        cp.wait_send()
-    local.wait()
+    def onward(p):
+        for q in xpeers:
+            piece = w_ref.at[q, p, c]
+            remote(piece, piece, xsend, xrecv.at[q, p], sib).wait_recv()
+        row = w_ref.at[:, p, c]
+        remote(row, row, csend, crecv, sib).start()
+
+    for n, p in enumerate(ypeers):
+        piece = w_ref.at[x, p, c]
+        remote(piece, piece, ysend, yrecv.at[p], sib).wait_recv()
+        for q in xpeers:
+            remote(piece, piece, xsend, xrecv.at[x, p], device(q, z, y, c)).start()
+        if n >= 2:
+            onward(ypeers[n - 2])
+    onward(ypeers[5])
+    onward(ypeers[6])
+    half = w_ref.at[:, pl.ds(0, 4)]
+    remote(half, half, csend, crecv, sib).wait()
+    seven = w_ref.at[0, pl.ds(0, 7), 0]
+    remote(seven, seven, ysend, yrecv.at[0], sib).wait_send()
+    more = w_ref.at[pl.ds(0, 3), pl.ds(0, 7), 0]
+    remote(more, more, xsend, yrecv.at[0], sib).wait_send()
 
 
 def main_kernel(
-    w_ref, hid_ref, gm_ref, doc_ref, nb_ref, irms_ref, cos_ref, sin_ref,
+    w_ref, hid_hbm, gm_hbm, nb_ref, irms_ref, cos_ref, sin_ref, mask_ref,
     mixed_ref, gh_ref, gout_ref,
-    mixbuf, ghbuf, pin, pout, cin, cout, xin, xout, xrin, xrout, ybuf, yrbuf, msg, rbuf,
+    hid_ref, gm_ref, pin, pout, cin, cout, xin, xout, xrin, xrout, ybuf, yrbuf, msg, rbuf,
     cs, cr, xs, xr, ys, yr, fs, fr, ls,
 ):
     x, z, y, c = coords()
@@ -140,25 +170,32 @@
     def _():
         signal(barrier, device(x, z, sy, sc))
 
+    gm_load = pltpu.make_async_copy(gm_hbm, gm_ref, ls.at[0])
+    gm_load.start()
+    hid_load = pltpu.make_async_copy(hid_hbm, hid_ref, ls.at[1])
+    hid_load.start()
+
     lo = lanes((TOK, 128)) < 64
     cos, sin = cos_ref[...], sin_ref[...]
     grad_scale = 131072 ** (-0.5)
     zero = jnp.zeros((TOK, 128), F32)
 
-    proj = jnp.dot(nb_ref[...], w_ref[:, :640], preferred_element_type=F32)
+    nb = nb_ref[...]
+    proj = [jnp.dot(nb, w_ref[t], preferred_element_type=F32) for t in range(2)]
+    proj.append(jnp.dot(nb, w_ref[2, :, :128], preferred_element_type=F32))
     q = []
     for t in range(4):
-        v = proj[:, 128 * t : 128 * t + 128]
+        v = proj[t // 2][:, 128 * (t % 2) : 128 * (t % 2) + 128]
         q.append(v * cos + swap_halves(v) * sin)
     k_hi = jnp.where(lo, zero, q[3])
     k_lo = pltpu.roll(k_hi, 64, 1)
     q[3] = jnp.where(lo, q[3], zero)
     qb = [v.astype(BF16) for v in q]
     kk = jnp.concatenate([k_lo.astype(BF16), k_hi.astype(BF16)], axis=0)
-    v_lo = jnp.where(lo, proj[:, 512:640], zero)
+    v_lo = jnp.where(lo, proj[2], zero)
     v_hi = pltpu.roll(v_lo, 64, 1)
     vv = jnp.concatenate([v_lo.astype(BF16), v_hi.astype(BF16)], axis=0)
-    allowed = allowed_pairs(doc_ref)
+    allowed = mask_ref[...] > 0.5
     probs, pb = [], []
     for t in range(4):
         s2 = lax.dot_general(qb[t], kk if t < 3 else kk[:128], NT, preferred_element_type=F32)
@@ -173,6 +210,7 @@
         pair = jnp.concatenate([pb[2 * t - 1], pb[2 * t]], axis=1)
         att.append(jnp.dot(pair, vv, preferred_element_type=F32).astype(BF16))
     a = jnp.concatenate(att, axis=1)
+    gm_load.wait()
     gm = gm_ref[...]
     part = lax.dot_general(a, gm, TN, preferred_element_type=F32)
     for h in range(2):
@@ -187,8 +225,8 @@
         cp.start()
         copies.append(cp)
 
-    ga = jnp.dot(gm, w_ref[:, 512:], preferred_element_type=F32)
-    g = [ga[:, 128 * t : 128 * t + 128] for t in range(4)]
+    ga = [jnp.dot(gm, w_ref[t], preferred_element_type=F32) for t in (2, 3)]
+    g = [ga[t // 2][:, 128 * (t % 2) : 128 * (t % 2) + 128] for t in range(4)]
     g[0] = jnp.where(lo, zero, g[0])
     gb = [v.astype(BF16) for v in g]
     gs = [None] * 7
@@ -223,7 +261,7 @@
         tiles.append((v * cos - swap_halves(v) * sin).astype(BF16))
     tiles.append(jnp.where(lo, gv, zero).astype(BF16))
     gpa = jnp.concatenate(tiles, axis=1)
-    part = lax.dot_general(nb_ref[...], gpa, TN, preferred_element_type=F32)
+    part = lax.dot_general(nb, gpa, TN, preferred_element_type=F32)
     for h in range(2):
         for p in range(NX):
             r = 224 * p + 112 * h
@@ -258,17 +296,16 @@
         else:
             sum_in = s
 
-    out = lax.dot_general(a, w_ref[:, 512:], NT, preferred_element_type=F32)
-    mixbuf[...] = (hid_ref[...].astype(F32) + out).astype(BF16)
-    mix_copy = pltpu.make_async_copy(mixbuf, mixed_ref, ls.at[0])
-    mix_copy.start()
-    gn = lax.dot_general(gpa, w_ref[:, :640], NT, preferred_element_type=F32)
+    hid_load.wait()
+    hid = hid_ref[...].astype(F32)
+    out = sum(lax.dot_general(a[:, 256 * t : 256 * t + 256], w_ref[2 + t], NT, preferred_element_type=F32) for t in range(2))
+    mixed_ref[...] = (hid + out).astype(BF16)
+    gn = sum(lax.dot_general(gpa[:, 256 * t : 256 * t + 256], w_ref[t], NT, preferred_element_type=F32) for t in range(2))
+    gn = gn + lax.dot_general(gpa[:, 512:], w_ref[2, :, :128], NT, preferred_element_type=F32)
     irms = irms_ref[:, :1]
-    normed = hid_ref[...].astype(F32) * irms
+    normed = hid * irms
     mean = jnp.mean(gn * normed, axis=1, keepdims=True)
-    ghbuf[...] = ((gn - normed * mean) * irms + gm.astype(F32)).astype(BF16)
-    gh_copy = pltpu.make_async_copy(ghbuf, gh_ref, ls.at[1])
-    gh_copy.start()
+    gh_ref[...] = ((gn - normed * mean) * irms + gm.astype(F32)).astype(BF16)
 
     for p in xpeers:
         remote(xout.at[0], xrout.at[p], xs.at[0], xr.at[p], sib).wait_recv()
@@ -336,37 +373,51 @@
     for k in range(1, 16):
         s = lax.rem(z + k, 16)
         remote(msg.at[0], rbuf.at[s], fs.at[0], fr.at[s], sib).wait_recv()
-    gout_ref[...] = jnp.sum(rbuf[...], axis=0)
+    total = jnp.sum(rbuf[...], axis=0)
+    for t in range(8):
+        gout_ref[:, 128 * t : 128 * t + 128] = total[t : t + 1]
     for cp in copies:
         cp.wait_send()
-    mix_copy.wait()
-    gh_copy.wait()
+
+
+def write_kernel(mixed_ref, gh_ref, grads_ref, mixed_out, gh_out, in_out, out_out, sem):
+    copies = [pltpu.make_async_copy(mixed_ref, mixed_out, sem.at[0]), pltpu.make_async_copy(gh_ref, gh_out, sem.at[1])]
+    for cp in copies:
+        cp.start()
+    flat = grads_ref[...]
+    in_out[...] = flat[:, :504]
+    out_out[...] = pltpu.roll(flat, 520, 1)[:, :392]
+    for cp in copies:
+        cp.wait()
 
 
 def body(hidden_in, doc_ids, grad_mixed, in_codes, in_scales, out_codes, out_scales):
-    codes = jnp.concatenate([in_codes, out_codes.T], axis=1)
-    scales = jnp.repeat(jnp.concatenate([in_scales, out_scales.T], axis=1), HS, axis=1)
     vm = pl.BlockSpec(memory_space=VMEM)
-    anyspace = pl.BlockSpec(memory_space=pl.ANY)
+    hbm = pl.BlockSpec(memory_space=pltpu.HBM)
     dma = pltpu.SemaphoreType.DMA
     sds = jax.ShapeDtypeStruct
-    w, nb, irms, cos, sin = pl.pallas_call(
+    tokens = sds((TOK, D), BF16)
+    square = sds((TOK, 128), F32)
+    held = [pltpu.with_memory_space_constraint(v, pltpu.HBM) for v in (in_codes, out_codes.T, in_scales.T, out_scales, hidden_in, doc_ids)]
+    grad_mixed = pltpu.with_memory_space_constraint(grad_mixed, pltpu.HBM)
+    w, nb, irms, cos, sin, mask = pl.pallas_call(
         gather_kernel,
-        out_shape=(
-            sds((16, 56, 1024), BF16), sds((TOK, D), BF16), sds((TOK, 128), F32),
-            sds((TOK, 128), F32), sds((TOK, 128), F32),
-        ),
-        in_specs=[vm] * 4,
-        out_specs=(anyspace, vm, vm, vm, vm),
-        scratch_shapes=[VMEM((56, 1024), BF16), dma((7,)), dma((8,)), dma((8,)), dma((8,)), dma],
+        out_shape=(sds((4, 8, 2, 56, 256), BF16), tokens, square, square, square, square),
+        in_specs=[hbm] * 6,
+        out_specs=(vm,) * 6,
+        scratch_shapes=[
+            VMEM((56, 576), BF16), VMEM((56, 448), BF16), VMEM((9, 28), F32), VMEM((7, 28), F32),
+            VMEM((TOK, D), BF16), VMEM((1, 128), jnp.int32), VMEM((56, 128), F32),
+            dma((6,)), dma, dma((8,)), dma, dma((4, 8)), dma, dma,
+        ],
         compiler_params=pltpu.CompilerParams(collective_id=0, has_side_effects=True, vmem_limit_bytes=16 << 20),
         name="gather",
-    )(codes, scales, hidden_in, doc_ids)
+    )(*held)
     mixed, grad_hidden, grads = pl.pallas_call(
         main_kernel,
-        out_shape=(sds((TOK, D), BF16), sds((TOK, D), BF16), sds((8, 128), F32)),
-        in_specs=[vm] * 8,
-        out_specs=(anyspace, anyspace, vm),
+        out_shape=(tokens, tokens, sds((1, 1024), F32)),
+        in_specs=[vm, hbm, hbm] + [vm] * 5,
+        out_specs=(vm, vm, vm),
         scratch_shapes=[
             VMEM((TOK, D), BF16), VMEM((TOK, D), BF16),
             VMEM((2, 4, 112, 640), BF16), VMEM((2, 4, 56, 896), BF16),
@@ -379,9 +430,16 @@
         ],
         compiler_params=pltpu.CompilerParams(collective_id=1, has_side_effects=True, vmem_limit_bytes=32 << 20),
         name="sublayer",
-    )(w.reshape(D, 1024), hidden_in, grad_mixed, doc_ids, nb, irms, cos, sin)
-    flat = grads.reshape(1024)
-    return mixed, grad_hidden, flat[:504], flat[504:896]
+    )(w.reshape(4, D, 256), held[4], grad_mixed, nb, irms, cos, sin, mask)
+    mixed, grad_hidden, grad_in, grad_out = pl.pallas_call(
+        write_kernel,
+        out_shape=(pltpu.HBM((TOK, D), BF16), pltpu.HBM((TOK, D), BF16), pltpu.HBM((1, 504), F32), pltpu.HBM((1, 392), F32)),
+        in_specs=[vm] * 3,
+        out_specs=(hbm, hbm, pl.BlockSpec(), pl.BlockSpec()),
+        scratch_shapes=[dma((2,))],
+        name="write",
+    )(*(pltpu.with_memory_space_constraint(v, VMEM) for v in (mixed, grad_hidden, grads)))
+    return mixed, grad_hidden, grad_in.reshape(504), grad_out.reshape(392)
 
 
 def solution(mesh):

time: 95.9 us -> 81.4 us (0.85)
  local copies, waits for them, and re-layouts: 7.04 us -> 0 us
  Pallas kernels: 84.6 us -> 79.5 us
  other arithmetic: 1.73 us -> 0 us
    unnamed x12 -> x0, local copies, waits for them, and re-layouts: 5.49 us -> none
    pallas_call x2 -> x3, Pallas kernels: 84.6 us -> 79.5 us  [the longest x1 47.2 us: body(): pl.pallas_call(main_kernel, out_shape=(tokens, tokens, sds((1, 1024), F32...]
    concatenate x2 -> x0, other arithmetic: 1.73 us -> none  [the longest x1 1.01 us: body(): codes = jnp.concatenate([in_codes, out_codes.T], axis=1)]
    slice x2 -> x0, local copies, waits for them, and re-layouts: 1.23 us -> none  [body(): return (mixed, grad_hidden, flat[:504], flat[504:896])]
where the time goes in v2:
time: 81.4 us; the launch traced here: 80.2 us
  Pallas kernels  79.5 us (98%)
    pallas_call x1, Pallas kernels, body(): pl.pallas_call(main_kernel, out_shape=(tokens, tokens, sds((1, 1024), F32...  47.2 us
    pallas_call x1, Pallas kernels, body(): pl.pallas_call(gather_kernel, out_shape=(sds((4, 8, 2, 56, 256), BF16), t...  31 us

profile of v2, /device:TPU:1, one launch (start us, length us, event | category | flops | bytes accessed | tf_op | source)
XLA Modules:
  0.0 80.2 jit_solution(17425392965170248751)
XLA Ops:
  0.6 31.0 %gather.1 = (bf16[4,8,2,56,256]{4,3,2,1,0:T(8,128)(2,1)S(1)}, bf16[128,896]{1,0:T(8,128)(2,1)S(1)}, f32[128,128]{1,0:T(8,128)S(1)}, f32[128,128]{1,0:T(8,128)S(1...) custom-call(bf16[56,576]{1,0:T(8,128)(2,1)} %inc_ref.1, bf16[56,448]{1,0:T(8,128)(2,1)} %bitcast.6, f32[9,28]{1,0:T(8,128)} %bitcast.7, ...), custom_call_target="tpu_custom_call" | custom-call | tf_op jit(solution)/shard_map/gather/pallas_call | solution.py:403
  31.6 47.2 %sublayer.1 = (bf16[128,896]{1,0:T(8,128)(2,1)S(1)}, bf16[128,896]{1,0:T(8,128)(2,1)S(1)}, f32[1,1024]{1,0:T(1,128)S(1)}) custom-call(bf16[4,896,256]{2,1,0:T(8,128)(2,1)S(1)} %bitcast.5, bf16[128,896]{1,0:T(8,128)(2,1)} %hid_hbm.1, bf16[128,896]{1,0:T(8,128)(2,1)} %gm_hbm.1, bf16[128,896]{1,0:T(8,128)(2,1)S(1)} %get-tuple-element.18.nb_ref, ...), custom_call_target="tpu_custom_call" | custom-call | tf_op jit(solution)/shard_map/sublayer/pallas_call | solution.py:416
  78.8 1.4 %write.1 = (bf16[128,896]{1,0:T(8,128)(2,1)}, bf16[128,896]{1,0:T(8,128)(2,1)}, f32[1,504]{1,0:T(1,128)}, f32[1,392]{1,0:T(1,128)}) custom-call(bf16[128,896]{1,0:T(8,128)(2,1)S(1)} %get-tuple-element.23.mixed_ref, bf16[128,896]{1,0:T(8,128)(2,1)S(1)} %get-tuple-element.24.gh_ref, f32[1,1024]{1,0:T(1,128)S(1)} %get-tuple-element.25.grads_ref), custom_call_target="tpu_custom_call" | custom-call | tf_op jit(solution)/shard_map/write/pallas_call | solution.py:434

commit v3 on v2

--- a/solution.py
+++ b/solution.py
@@ -146,7 +146,7 @@
 def main_kernel(
     w_ref, hid_hbm, gm_hbm, nb_ref, irms_ref, cos_ref, sin_ref, mask_ref,
     mixed_ref, gh_ref, gout_ref,
-    hid_ref, gm_ref, pin, pout, cin, cout, xin, xout, xrin, xrout, ybuf, yrbuf, msg, rbuf,
+    hid_ref, gm_ref, pin, pout, cin, cout, xin, xout, xrin, xrout, yout, yrout, ybuf, yrbuf, msg, rbuf,
     cs, cr, xs, xr, ys, yr, fs, fr, ls,
 ):
     x, z, y, c = coords()
@@ -212,15 +212,19 @@
     a = jnp.concatenate(att, axis=1)
     gm_load.wait()
     gm = gm_ref[...]
-    part = lax.dot_general(a, gm, TN, preferred_element_type=F32)
+    src, dst = lanes((512, 512), 0), lanes((512, 512))
+    want = 64 + 112 * ((dst >> 3) & 3) + 56 * (dst >> 8) + 7 * ((dst >> 5) & 7) + (dst & 7)
+    order = jnp.where((src == want) & ((dst & 7) < 7), 1.0, 0.0).astype(BF16)
+    ordered = jnp.dot(a, order, preferred_element_type=F32).astype(BF16)
+    part = lax.dot_general(ordered, gm, TN, preferred_element_type=F32)
     for h in range(2):
-        for p in range(NX):
-            r = 64 + 112 * p + 56 * h
-            pout[h, p] = (part[r : r + 56] * grad_scale).astype(BF16)
+        for p in range(NY):
+            r = 256 * h + 32 * p
+            pout[h, p] = (part[r : r + 32] * grad_scale).astype(BF16)
     pl.semaphore_wait(barrier, 27 - diagonal.astype(jnp.int32))
     copies = []
-    for k in range(NX):
-        p = lax.rem(x + 1 + k, NX)
+    for k in range(NY):
+        p = lax.rem(y + 1 + k, NY)
         cp = remote(pout.at[1 - c, p], cout.at[p], cs.at[k], cr.at[p], sib)
         cp.start()
         copies.append(cp)
@@ -268,29 +272,29 @@
             pin[h, p] = (part[r : r + 112] * grad_scale).astype(BF16)
     for k in range(NX):
         p = lax.rem(x + 1 + k, NX)
-        cp = remote(pin.at[1 - c, p], cin.at[p], cs.at[4 + k], cr.at[4 + p], sib)
+        cp = remote(pin.at[1 - c, p], cin.at[p], cs.at[8 + k], cr.at[8 + p], sib)
         cp.start()
         copies.append(cp)
 
     sum_out = sum_in = None
-    for k in range(NX):
-        p = lax.rem(x + 1 + k, NX)
+    for k in range(NY):
+        p = lax.rem(y + 1 + k, NY)
         remote(pout.at[c, p], cout.at[p], cs.at[0], cr.at[p], sib).wait_recv()
         s = pout[c, p].astype(F32) + cout[p].astype(F32)
-        if k < NX - 1:
-            xout[k] = s.astype(BF16)
-            cp = remote(xout.at[k], xrout.at[x], xs.at[k], xr.at[x], device(p, z, y, c))
+        if k < NY - 1:
+            yout[k] = s.astype(BF16)
+            cp = remote(yout.at[k], yrout.at[y], ys.at[8 + k], yr.at[8 + y], device(x, z, p, c))
             cp.start()
             copies.append(cp)
         else:
             sum_out = s
     for k in range(NX):
         p = lax.rem(x + 1 + k, NX)
-        remote(pin.at[c, p], cin.at[p], cs.at[0], cr.at[4 + p], sib).wait_recv()
+        remote(pin.at[c, p], cin.at[p], cs.at[0], cr.at[8 + p], sib).wait_recv()
         s = pin[c, p].astype(F32) + cin[p].astype(F32)
         if k < NX - 1:
             xin[k] = s.astype(BF16)
-            cp = remote(xin.at[k], xrin.at[x], xs.at[4 + k], xr.at[4 + x], device(p, z, y, c))
+            cp = remote(xin.at[k], xrin.at[x], xs.at[k], xr.at[x], device(p, z, y, c))
             cp.start()
             copies.append(cp)
         else:
@@ -308,37 +312,46 @@
     gh_ref[...] = ((gn - normed * mean) * irms + gm.astype(F32)).astype(BF16)
 
     for p in xpeers:
-        remote(xout.at[0], xrout.at[p], xs.at[0], xr.at[p], sib).wait_recv()
-        sum_out = sum_out + xrout[p].astype(F32)
-    high = lanes((56, 512)) >= 64
+        remote(xin.at[0], xrin.at[p], xs.at[0], xr.at[p], sib).wait_recv()
+        sum_in = sum_in + xrin[p].astype(F32)
+    row, col = lanes((128, 112), 0), lanes((128, 112))
+    pick_in = ((row & 7) < 7) & (col == 7 * (row >> 3) + (row & 7))
+    e_in = jnp.where(pick_in, 1.0, 0.0).astype(BF16)
+    y_in = jnp.dot(e_in, sum_in.astype(BF16), preferred_element_type=F32)
+    for p in range(NY):
+        ybuf[p] = y_in[16 * p : 16 * p + 16].astype(BF16)
+    for k, p in enumerate(ypeers):
+        cp = remote(ybuf.at[p], yrbuf.at[y], ys.at[k], yr.at[y], device(x, z, p, c))
+        cp.start()
+        copies.append(cp)
+
+    for p in ypeers:
+        remote(yout.at[0], yrout.at[p], ys.at[0], yr.at[8 + p], sib).wait_recv()
+        sum_out = sum_out + yrout[p].astype(F32)
+    for p in range(NX):
+        xout[p] = sum_out[8 * p : 8 * p + 8]
+    for k, p in enumerate(xpeers):
+        cp = remote(xout.at[p], xrout.at[x], xs.at[4 + k], xr.at[4 + x], device(p, z, y, c))
+        cp.start()
+        copies.append(cp)
+    sum_out = xout[x]
+    for p in xpeers:
+        remote(xout.at[0], xrout.at[p], xs.at[0], xr.at[4 + p], sib).wait_recv()
+        sum_out = sum_out + xrout[p]
+    high = lanes((8, 512)) >= 64
     left = jnp.where(high, pltpu.roll(sum_out[:, :512], 64, 1), 0.0)
     right = jnp.where(high, sum_out[:, 384:], 0.0)
     halves = jnp.concatenate([left, right], axis=0).astype(BF16)
-    row, col = lanes((128, 112), 0), lanes((128, 112))
-    j = row & 7
-    q7 = 7 * ((row >> 3) & 1) + j
-    pick_out = (j < 7) & (col == 7 * (row >> 4) + (q7 >> 1) + 56 * (q7 & 1))
-    pick_in = (j < 7) & (col == 7 * (row >> 3) + j)
-    e_out = jnp.where(pick_out, 1.0, 0.0).astype(BF16)
-    e_in = jnp.where(pick_in, 1.0, 0.0).astype(BF16)
+    row, col = lanes((16, 16), 0), lanes((16, 16))
+    q7 = 7 * (row >> 3) + (row & 7)
+    e_out = jnp.where(((row & 7) < 7) & (col == (q7 >> 1) + 8 * (q7 & 1)), 1.0, 0.0).astype(BF16)
     y_out = jnp.dot(e_out, halves, preferred_element_type=F32)
-    for p in xpeers:
-        remote(xin.at[0], xrin.at[p], xs.at[0], xr.at[4 + p], sib).wait_recv()
-        sum_in = sum_in + xrin[p].astype(F32)
-    y_in = jnp.dot(e_in, sum_in.astype(BF16), preferred_element_type=F32)
-    for p in range(NY):
-        rows = slice(16 * p, 16 * p + 16)
-        ybuf[p, :, :512] = y_in[rows, :512].astype(BF16)
-        ybuf[p, :, 512:640] = (y_in[rows, 512:] + y_out[rows, :128]).astype(BF16)
-        ybuf[p, :, 640:] = y_out[rows, 128:].astype(BF16)
-    for k, p in enumerate(ypeers):
-        cp = remote(ybuf.at[p], yrbuf.at[y], ys.at[k], yr.at[y], device(x, z, p, c))
-        cp.start()
-        copies.append(cp)
+
     total = ybuf[y].astype(F32)
     for p in ypeers:
         remote(ybuf.at[0], yrbuf.at[p], ys.at[0], yr.at[p], sib).wait_recv()
         total = total + yrbuf[p].astype(F32)
+    total = jnp.concatenate([total[:, :512], total[:, 512:] + y_out[:, :128], y_out[:, 128:]], axis=1)
 
     before = pltpu.roll(total, 1, 0)
     lane = lanes((16, 1024))
@@ -350,7 +363,7 @@
         old = (lane < 72 * k) | ((lane >= 504) & (lane < 504 + 56 * k))
         flat = jnp.where(jrow == k, jnp.where(old, past, here), flat)
     for t in range(8):
-        msg[:, t, :] = flat[:, 128 * t : 128 * t + 128]
+        msg[:, t, :] = flat[:, 128 * t : 128 * t + 128].astype(BF16)
     for k in range(1, 16):
         i = lax.rem(me + k, 16)
         cp = remote(msg.at[i], rbuf.at[z], fs.at[k], fr.at[z], device(x, owner, lax.div(i, 2), lax.rem(i, 2)))
@@ -373,7 +386,7 @@
     for k in range(1, 16):
         s = lax.rem(z + k, 16)
         remote(msg.at[0], rbuf.at[s], fs.at[0], fr.at[s], sib).wait_recv()
-    total = jnp.sum(rbuf[...], axis=0)
+    total = jnp.sum(rbuf[...].astype(F32), axis=0)
     for t in range(8):
         gout_ref[:, 128 * t : 128 * t + 128] = total[t : t + 1]
     for cp in copies:
@@ -420,13 +433,14 @@
         out_specs=(vm, vm, vm),
         scratch_shapes=[
             VMEM((TOK, D), BF16), VMEM((TOK, D), BF16),
-            VMEM((2, 4, 112, 640), BF16), VMEM((2, 4, 56, 896), BF16),
-            VMEM((4, 112, 640), BF16), VMEM((4, 56, 896), BF16),
-            VMEM((3, 112, 640), BF16), VMEM((3, 56, 896), BF16),
-            VMEM((4, 112, 640), BF16), VMEM((4, 56, 896), BF16),
-            VMEM((8, 16, 1024), BF16), VMEM((8, 16, 1024), BF16),
-            VMEM((16, 8, 128), F32), VMEM((16, 8, 128), F32),
-            dma((8,)), dma((8,)), dma((8,)), dma((8,)), dma((7,)), dma((8,)), dma((16,)), dma((16,)), dma((3,)),
+            VMEM((2, 4, 112, 640), BF16), VMEM((2, 8, 32, 896), BF16),
+            VMEM((4, 112, 640), BF16), VMEM((8, 32, 896), BF16),
+            VMEM((3, 112, 640), BF16), VMEM((4, 8, 896), F32),
+            VMEM((4, 112, 640), BF16), VMEM((4, 8, 896), F32),
+            VMEM((7, 32, 896), BF16), VMEM((8, 32, 896), BF16),
+            VMEM((8, 16, 640), BF16), VMEM((8, 16, 640), BF16),
+            VMEM((16, 8, 128), BF16), VMEM((16, 8, 128), BF16),
+            dma((12,)), dma((12,)), dma((8,)), dma((8,)), dma((15,)), dma((16,)), dma((16,)), dma((16,)), dma((3,)),
         ],
         compiler_params=pltpu.CompilerParams(collective_id=1, has_side_effects=True, vmem_limit_bytes=32 << 20),
         name="sublayer",

time: 81.4 us -> 75.2 us (0.924); the launches traced: 80.2 us -> 74.9 us
  Pallas kernels: 79.5 us -> 74.3 us
    pallas_call x1, Pallas kernels: 47.2 us -> 42 us  [body(): pl.pallas_call(main_kernel, out_shape=(tokens, tokens, sds((1, 1024), F32...]
where the time goes in v3:
time: 75.2 us; the launch traced here: 74.9 us
  Pallas kernels  74.3 us (99%)
    pallas_call x1, Pallas kernels, body(): pl.pallas_call(main_kernel, out_shape=(tokens, tokens, sds((1, 1024), F32...  42 us
    pallas_call x1, Pallas kernels, body(): pl.pallas_call(gather_kernel, out_shape=(sds((4, 8, 2, 56, 256), BF16), t...  31 us

profile of v3, /device:TPU:1, one launch (start us, length us, event | category | flops | bytes accessed | tf_op | source)
XLA Modules:
  0.0 74.9 jit_solution(5862782698728305697)
XLA Ops:
  0.6 31.0 %gather.1 = (bf16[4,8,2,56,256]{4,3,2,1,0:T(8,128)(2,1)S(1)}, bf16[128,896]{1,0:T(8,128)(2,1)S(1)}, f32[128,128]{1,0:T(8,128)S(1)}, f32[128,128]{1,0:T(8,128)S(1...) custom-call(bf16[56,576]{1,0:T(8,128)(2,1)} %inc_ref.1, bf16[56,448]{1,0:T(8,128)(2,1)} %bitcast.6, f32[9,28]{1,0:T(8,128)} %bitcast.7, ...), custom_call_target="tpu_custom_call" | custom-call | tf_op jit(solution)/shard_map/gather/pallas_call | solution.py:416
  31.6 42.0 %sublayer.1 = (bf16[128,896]{1,0:T(8,128)(2,1)S(1)}, bf16[128,896]{1,0:T(8,128)(2,1)S(1)}, f32[1,1024]{1,0:T(1,128)S(1)}) custom-call(bf16[4,896,256]{2,1,0:T(8,128)(2,1)S(1)} %bitcast.5, bf16[128,896]{1,0:T(8,128)(2,1)} %hid_hbm.1, bf16[128,896]{1,0:T(8,128)(2,1)} %gm_hbm.1, bf16[128,896]{1,0:T(8,128)(2,1)S(1)} %get-tuple-element.18.nb_ref, ...), custom_call_target="tpu_custom_call" | custom-call | tf_op jit(solution)/shard_map/sublayer/pallas_call | solution.py:429
  73.6 1.4 %write.1 = (bf16[128,896]{1,0:T(8,128)(2,1)}, bf16[128,896]{1,0:T(8,128)(2,1)}, f32[1,504]{1,0:T(1,128)}, f32[1,392]{1,0:T(1,128)}) custom-call(bf16[128,896]{1,0:T(8,128)(2,1)S(1)} %get-tuple-element.23.mixed_ref, bf16[128,896]{1,0:T(8,128)(2,1)S(1)} %get-tuple-element.24.gh_ref, f32[1,1024]{1,0:T(1,128)S(1)} %get-tuple-element.25.grads_ref), custom_call_target="tpu_custom_call" | custom-call | tf_op jit(solution)/shard_map/write/pallas_call | solution.py:448

commit v4 on v3

--- a/solution.py
+++ b/solution.py
@@ -12,6 +12,7 @@
 D, HEADS, HS = 896, 7, 64
 TOK = 128
 NX, NZ, NY = 4, 16, 8
+NEAR = 2
 ROPE_BASE = 1000000.0
 EPS = 1e-06
 VMEM = pltpu.VMEM
@@ -56,13 +57,14 @@
 def gather_kernel(
     inc_ref, outc_ref, ins_ref, outs_ref, hid_ref, doc_ref,
     w_ref, nb_ref, irms_ref, cos_ref, sin_ref, mask_ref,
-    ic, oc, ins, outs, hid, doc, pad, lsem, ysend, yrecv, xsend, xrecv, csend, crecv,
+    ic, oc, ins, outs, hid, doc, pad, lsem, ysend, nsend, yrecv, xsend, xrecv, csend, crecv,
 ):
     x, z, y, c = coords()
     me = 2 * y + c
     sib = device(x, z, y, 1 - c)
     xpeers = [lax.rem(x + k, NX) for k in (1, 3, 2)]
     ypeers = [lax.rem(y + k, NY) for k in (1, 7, 2, 6, 3, 5, 4)]
+    near, far = ypeers[:NEAR], ypeers[NEAR:]
     barrier = pltpu.get_barrier_semaphore()
     for p in ypeers:
         signal(barrier, device(x, z, p, c))
@@ -98,9 +100,11 @@
 
     pl.semaphore_wait(barrier, 11)
     mine = w_ref.at[x, y, c]
-    for k, p in enumerate(ypeers):
+    whole = w_ref.at[:, y, c]
+    for p in far:
         remote(mine, mine, ysend, yrecv.at[y], device(x, z, p, c)).start()
-    whole = w_ref.at[:, y, c]
+    for p in near:
+        remote(whole, whole, nsend, yrecv.at[y], device(x, z, p, c)).start()
     remote(whole, whole, csend, crecv, sib).start()
 
     loads[4].wait()
@@ -119,28 +123,35 @@
     sine = jnp.sin(angle)
     sin_ref[...] = jnp.where((lane & 63) < 32, -sine, sine)
 
+    def share(p):
+        row = w_ref.at[:, p, c]
+        remote(row, row, csend, crecv, sib).start()
+
     def onward(p):
         for q in xpeers:
             piece = w_ref.at[q, p, c]
             remote(piece, piece, xsend, xrecv.at[q, p], sib).wait_recv()
-        row = w_ref.at[:, p, c]
-        remote(row, row, csend, crecv, sib).start()
-
-    for n, p in enumerate(ypeers):
+        share(p)
+
+    for p in far:
         piece = w_ref.at[x, p, c]
         remote(piece, piece, ysend, yrecv.at[p], sib).wait_recv()
         for q in xpeers:
             remote(piece, piece, xsend, xrecv.at[x, p], device(q, z, y, c)).start()
-        if n >= 2:
-            onward(ypeers[n - 2])
-    onward(ypeers[5])
-    onward(ypeers[6])
+    for n, p in enumerate(far):
+        onward(p)
+        if n < NEAR:
+            row = w_ref.at[:, near[n], c]
+            remote(row, row, ysend, yrecv.at[near[n]], sib).wait_recv()
+            share(near[n])
     half = w_ref.at[:, pl.ds(0, 4)]
     remote(half, half, csend, crecv, sib).wait()
-    seven = w_ref.at[0, pl.ds(0, 7), 0]
-    remote(seven, seven, ysend, yrecv.at[0], sib).wait_send()
-    more = w_ref.at[pl.ds(0, 3), pl.ds(0, 7), 0]
-    remote(more, more, xsend, yrecv.at[0], sib).wait_send()
+    sent = w_ref.at[0, pl.ds(0, 7 - NEAR), 0]
+    remote(sent, sent, ysend, yrecv.at[0], sib).wait_send()
+    sent = w_ref.at[:, pl.ds(0, NEAR), 0]
+    remote(sent, sent, nsend, yrecv.at[0], sib).wait_send()
+    sent = w_ref.at[pl.ds(0, 3), pl.ds(0, 7 - NEAR), 0]
+    remote(sent, sent, xsend, yrecv.at[0], sib).wait_send()
 
 
 def main_kernel(
@@ -154,15 +165,15 @@
     sib = device(x, z, y, 1 - c)
     xpeers = [lax.rem(x + k, NX) for k in range(1, NX)]
     ypeers = [lax.rem(y + k, NY) for k in range(1, NY)]
-    owner = 8 * c + y
-    diagonal = z == owner
+    group, quad = lax.div(y, 4), lax.rem(y, 4)
+    sy, sc = 4 * group + lax.div(lax.rem(z, 8), 2), lax.div(z, 8)
+    diagonal = jnp.logical_and(sy == y, sc == c)
     barrier = pltpu.get_barrier_semaphore()
     signal(barrier, sib)
     for p in xpeers:
         signal(barrier, device(p, z, y, c))
     for p in ypeers:
         signal(barrier, device(x, z, p, c))
-    sy, sc = lax.rem(z, 8), lax.div(z, 8)
     for k in range(1, NZ):
         signal(barrier, device(x, lax.rem(z + k, NZ), sy, sc))
 
@@ -213,8 +224,9 @@
     gm_load.wait()
     gm = gm_ref[...]
     src, dst = lanes((512, 512), 0), lanes((512, 512))
-    want = 64 + 112 * ((dst >> 3) & 3) + 56 * (dst >> 8) + 7 * ((dst >> 5) & 7) + (dst & 7)
-    order = jnp.where((src == want) & ((dst & 7) < 7), 1.0, 0.0).astype(BF16)
+    block = 7 * (2 * ((dst >> 5) & 3) + ((dst >> 2) & 1)) + 3 * ((dst >> 7) & 1) + (dst & 3)
+    want = 64 + 112 * ((dst >> 3) & 3) + 56 * (dst >> 8) + block
+    order = jnp.where(src == want, 1.0, 0.0).astype(BF16)
     ordered = jnp.dot(a, order, preferred_element_type=F32).astype(BF16)
     part = lax.dot_general(ordered, gm, TN, preferred_element_type=F32)
     for h in range(2):
@@ -311,12 +323,15 @@
     mean = jnp.mean(gn * normed, axis=1, keepdims=True)
     gh_ref[...] = ((gn - normed * mean) * irms + gm.astype(F32)).astype(BF16)
 
+    row, col = lanes((128, 112), 0), lanes((128, 112))
+    from_row = 14 * (2 * ((row >> 4) & 3) + ((row >> 3) & 1)) + 7 * (row >> 6) + (row & 7)
+    e_in = jnp.where(((row & 7) < 7) & (col == from_row), 1.0, 0.0).astype(BF16)
+    row, col = lanes((16, 16), 0), lanes((16, 16))
+    turn = (row & 7) + group
+    e_out = jnp.where(((row & 7) < 7) & (col == 4 * (row >> 3) + (turn >> 1) + 8 * (turn & 1)), 1.0, 0.0).astype(BF16)
     for p in xpeers:
         remote(xin.at[0], xrin.at[p], xs.at[0], xr.at[p], sib).wait_recv()
         sum_in = sum_in + xrin[p].astype(F32)
-    row, col = lanes((128, 112), 0), lanes((128, 112))
-    pick_in = ((row & 7) < 7) & (col == 7 * (row >> 3) + (row & 7))
-    e_in = jnp.where(pick_in, 1.0, 0.0).astype(BF16)
     y_in = jnp.dot(e_in, sum_in.astype(BF16), preferred_element_type=F32)
     for p in range(NY):
         ybuf[p] = y_in[16 * p : 16 * p + 16].astype(BF16)
@@ -338,39 +353,45 @@
     for p in xpeers:
         remote(xout.at[0], xrout.at[p], xs.at[0], xr.at[4 + p], sib).wait_recv()
         sum_out = sum_out + xrout[p]
-    high = lanes((8, 512)) >= 64
-    left = jnp.where(high, pltpu.roll(sum_out[:, :512], 64, 1), 0.0)
-    right = jnp.where(high, sum_out[:, 384:], 0.0)
+    left, right = sum_out[:, :512], pltpu.roll(sum_out[:, 384:], 448, 1)
     halves = jnp.concatenate([left, right], axis=0).astype(BF16)
-    row, col = lanes((16, 16), 0), lanes((16, 16))
-    q7 = 7 * (row >> 3) + (row & 7)
-    e_out = jnp.where(((row & 7) < 7) & (col == (q7 >> 1) + 8 * (q7 & 1)), 1.0, 0.0).astype(BF16)
     y_out = jnp.dot(e_out, halves, preferred_element_type=F32)
+    before = pltpu.roll(y_out, 1, 0)
+    lane, jrow = lanes((16, 512)), lanes((16, 512), 0) & 7
+    flat_out = jnp.zeros((16, 512), F32)
+    for k in range(8):
+        old = lane < 56 * k + 120
+        here, past = pltpu.roll(y_out, (120 + 56 * k) % 512, 1), pltpu.roll(before, (184 + 56 * k) % 512, 1)
+        flat_out = jnp.where(jrow == k, jnp.where(old, past, here), flat_out)
 
     total = ybuf[y].astype(F32)
     for p in ypeers:
         remote(ybuf.at[0], yrbuf.at[p], ys.at[0], yr.at[p], sib).wait_recv()
         total = total + yrbuf[p].astype(F32)
-    total = jnp.concatenate([total[:, :512], total[:, 512:] + y_out[:, :128], y_out[:, 128:]], axis=1)
 
     before = pltpu.roll(total, 1, 0)
-    lane = lanes((16, 1024))
-    jrow = lanes((16, 1024), 0) & 7
-    flat = jnp.zeros((16, 1024), F32)
+    lane, jrow = lanes((16, 640)), lanes((16, 640), 0) & 7
+    flat_in = jnp.zeros((16, 640), F32)
     for k in range(8):
-        here = jnp.where(lane < 504, pltpu.roll(total, 72 * k, 1), pltpu.roll(total, (56 * k - 72) % 1024, 1))
-        past = jnp.where(lane < 504, pltpu.roll(before, (448 + 72 * k) % 1024, 1), pltpu.roll(before, (504 + 56 * k) % 1024, 1))
-        old = (lane < 72 * k) | ((lane >= 504) & (lane < 504 + 56 * k))
-        flat = jnp.where(jrow == k, jnp.where(old, past, here), flat)
+        here, past = pltpu.roll(total, 72 * k, 1), pltpu.roll(before, 64 + 72 * k, 1)
+        flat_in = jnp.where(jrow == k, jnp.where(lane < 72 * k, past, here), flat_in)
+    seam = jnp.where(lanes((16, 128)) < 120, flat_in[:, 384:512], flat_out[:, :128])
+    flat = jnp.concatenate([flat_in[:, :384], seam, flat_out[:, 128:], jnp.zeros((16, 128), F32)], axis=1)
     for t in range(8):
         msg[:, t, :] = flat[:, 128 * t : 128 * t + 128].astype(BF16)
+    own = 8 * lax.rem(z, 2) + lax.rem(me, 8)
+
+    def target(i):
+        n = lax.rem(i, 8)
+        return device(x, 8 * c + 2 * quad + lax.div(i, 8), 4 * group + lax.div(n, 2), lax.rem(n, 2))
+
     for k in range(1, 16):
-        i = lax.rem(me + k, 16)
-        cp = remote(msg.at[i], rbuf.at[z], fs.at[k], fr.at[z], device(x, owner, lax.div(i, 2), lax.rem(i, 2)))
+        i = lax.rem(own + k, 16)
+        cp = remote(msg.at[i], rbuf.at[z], fs.at[k], fr.at[z], target(i))
         cp.start()
         copies.append(cp)
-    mine = remote(msg.at[me], rbuf.at[z], fs.at[0], fr.at[z], device(x, owner, y, c))
-    kept = pltpu.make_async_copy(msg.at[me], rbuf.at[z], ls.at[2])
+    mine = remote(msg.at[own], rbuf.at[z], fs.at[0], fr.at[z], target(own))
+    kept = pltpu.make_async_copy(msg.at[own], rbuf.at[z], ls.at[2])
 
     @pl.when(diagonal)
     def _():
@@ -421,7 +442,7 @@
         scratch_shapes=[
             VMEM((56, 576), BF16), VMEM((56, 448), BF16), VMEM((9, 28), F32), VMEM((7, 28), F32),
             VMEM((TOK, D), BF16), VMEM((1, 128), jnp.int32), VMEM((56, 128), F32),
-            dma((6,)), dma, dma((8,)), dma, dma((4, 8)), dma, dma,
+            dma((6,)), dma, dma, dma((8,)), dma, dma((4, 8)), dma, dma,
         ],
         compiler_params=pltpu.CompilerParams(collective_id=0, has_side_effects=True, vmem_limit_bytes=16 << 20),
         name="gather",

time: 75.2 us -> 70.9 us (0.943)
  Pallas kernels: 74.3 us -> 70.1 us
    pallas_call x1, Pallas kernels: 31 us -> 26 us  [body(): pl.pallas_call(gather_kernel, out_shape=(sds((4, 8, 2, 56, 256), BF16), t...]
where the time goes in v4:
time: 70.9 us; the launch traced here: 70.7 us
  Pallas kernels  70.1 us (99%)
    pallas_call x1, Pallas kernels, body(): pl.pallas_call(main_kernel, out_shape=(tokens, tokens, sds((1, 1024), F32...  42.7 us
    pallas_call x1, Pallas kernels, body(): pl.pallas_call(gather_kernel, out_shape=(sds((4, 8, 2, 56, 256), BF16), t...  26 us

profile of v4, /device:TPU:1, one launch (start us, length us, event | category | flops | bytes accessed | tf_op | source)
XLA Modules:
  0.0 70.7 jit_solution(10517966983826412529)
XLA Ops:
  0.6 26.0 %gather.1 = (bf16[4,8,2,56,256]{4,3,2,1,0:T(8,128)(2,1)S(1)}, bf16[128,896]{1,0:T(8,128)(2,1)S(1)}, f32[128,128]{1,0:T(8,128)S(1)}, f32[128,128]{1,0:T(8,128)S(1...) custom-call(bf16[56,576]{1,0:T(8,128)(2,1)} %inc_ref.1, bf16[56,448]{1,0:T(8,128)(2,1)} %bitcast.6, f32[9,28]{1,0:T(8,128)} %bitcast.7, ...), custom_call_target="tpu_custom_call" | custom-call | tf_op jit(solution)/shard_map/gather/pallas_call | solution.py:437
  26.6 42.7 %sublayer.1 = (bf16[128,896]{1,0:T(8,128)(2,1)S(1)}, bf16[128,896]{1,0:T(8,128)(2,1)S(1)}, f32[1,1024]{1,0:T(1,128)S(1)}) custom-call(bf16[4,896,256]{2,1,0:T(8,128)(2,1)S(1)} %bitcast.5, bf16[128,896]{1,0:T(8,128)(2,1)} %hid_hbm.1, bf16[128,896]{1,0:T(8,128)(2,1)} %gm_hbm.1, bf16[128,896]{1,0:T(8,128)(2,1)S(1)} %get-tuple-element.18.nb_ref, ...), custom_call_target="tpu_custom_call" | custom-call | tf_op jit(solution)/shard_map/sublayer/pallas_call | solution.py:450
  69.3 1.4 %write.1 = (bf16[128,896]{1,0:T(8,128)(2,1)}, bf16[128,896]{1,0:T(8,128)(2,1)}, f32[1,504]{1,0:T(1,128)}, f32[1,392]{1,0:T(1,128)}) custom-call(bf16[128,896]{1,0:T(8,128)(2,1)S(1)} %get-tuple-element.23.mixed_ref, bf16[128,896]{1,0:T(8,128)(2,1)S(1)} %get-tuple-element.24.gh_ref, f32[1,1024]{1,0:T(1,128)S(1)} %get-tuple-element.25.grads_ref), custom_call_target="tpu_custom_call" | custom-call | tf_op jit(solution)/shard_map/write/pallas_call | solution.py:469

commit v5 on v4

--- a/solution.py
+++ b/solution.py
@@ -158,7 +158,7 @@
     w_ref, hid_hbm, gm_hbm, nb_ref, irms_ref, cos_ref, sin_ref, mask_ref,
     mixed_ref, gh_ref, gout_ref,
     hid_ref, gm_ref, pin, pout, cin, cout, xin, xout, xrin, xrout, yout, yrout, ybuf, yrbuf, msg, rbuf,
-    cs, cr, xs, xr, ys, yr, fs, fr, ls,
+    cs, cr, xs, xr, ys, yr, fs, fr, ls, relay,
 ):
     x, z, y, c = coords()
     me = 2 * y + c
@@ -174,13 +174,8 @@
         signal(barrier, device(p, z, y, c))
     for p in ypeers:
         signal(barrier, device(x, z, p, c))
-    for k in range(1, NZ):
-        signal(barrier, device(x, lax.rem(z + k, NZ), sy, sc))
-
-    @pl.when(jnp.logical_not(diagonal))
-    def _():
-        signal(barrier, device(x, z, sy, sc))
-
+    for k in (1, 2, 3, 4, 12, 13, 14, 15):
+        signal(barrier, device(x, lax.rem(z + k, NZ), y, c))
     gm_load = pltpu.make_async_copy(gm_hbm, gm_ref, ls.at[0])
     gm_load.start()
     hid_load = pltpu.make_async_copy(hid_hbm, hid_ref, ls.at[1])
@@ -233,7 +228,7 @@
         for p in range(NY):
             r = 256 * h + 32 * p
             pout[h, p] = (part[r : r + 32] * grad_scale).astype(BF16)
-    pl.semaphore_wait(barrier, 27 - diagonal.astype(jnp.int32))
+    pl.semaphore_wait(barrier, 19)
     copies = []
     for k in range(NY):
         p = lax.rem(y + 1 + k, NY)
@@ -312,6 +307,10 @@
         else:
             sum_in = s
 
+    for k in range(2):
+        up = device(x, lax.rem(z + 4 + 8 * k, NZ), y, c)
+        pl.semaphore_signal(relay.at[k], inc=1, device_id=up, device_id_type=MESH)
+
     hid_load.wait()
     hid = hid_ref[...].astype(F32)
     out = sum(lax.dot_general(a[:, 256 * t : 256 * t + 256], w_ref[2 + t], NT, preferred_element_type=F32) for t in range(2))
@@ -335,6 +334,8 @@
     y_in = jnp.dot(e_in, sum_in.astype(BF16), preferred_element_type=F32)
     for p in range(NY):
         ybuf[p] = y_in[16 * p : 16 * p + 16].astype(BF16)
+    for k in range(2):
+        pl.semaphore_wait(relay.at[k], 1)
     for k, p in enumerate(ypeers):
         cp = remote(ybuf.at[p], yrbuf.at[y], ys.at[k], yr.at[y], device(x, z, p, c))
         cp.start()
@@ -414,13 +415,16 @@
         cp.wait_send()
 
 
-def write_kernel(mixed_ref, gh_ref, grads_ref, mixed_out, gh_out, in_out, out_out, sem):
-    copies = [pltpu.make_async_copy(mixed_ref, mixed_out, sem.at[0]), pltpu.make_async_copy(gh_ref, gh_out, sem.at[1])]
-    for cp in copies:
+def write_kernel(mixed_ref, gh_ref, grads_ref, mixed_out, gh_out, in_out, out_out, part_in, part_out, sem):
+    pairs = ((mixed_ref, mixed_out), (gh_ref, gh_out), (part_in, in_out), (part_out, out_out))
+    copies = [pltpu.make_async_copy(src, dst, sem.at[k]) for k, (src, dst) in enumerate(pairs)]
+    for cp in copies[:2]:
         cp.start()
     flat = grads_ref[...]
-    in_out[...] = flat[:, :504]
-    out_out[...] = pltpu.roll(flat, 520, 1)[:, :392]
+    part_in[...] = flat[:, :504]
+    part_out[...] = pltpu.roll(flat, 520, 1)[:, :392]
+    for cp in copies[2:]:
+        cp.start()
     for cp in copies:
         cp.wait()
 
@@ -461,7 +465,7 @@
             VMEM((7, 32, 896), BF16), VMEM((8, 32, 896), BF16),
             VMEM((8, 16, 640), BF16), VMEM((8, 16, 640), BF16),
             VMEM((16, 8, 128), BF16), VMEM((16, 8, 128), BF16),
-            dma((12,)), dma((12,)), dma((8,)), dma((8,)), dma((15,)), dma((16,)), dma((16,)), dma((16,)), dma((3,)),
+            dma((12,)), dma((12,)), dma((8,)), dma((8,)), dma((15,)), dma((16,)), dma((16,)), dma((16,)), dma((3,)), pltpu.SemaphoreType.REGULAR((2,)),
         ],
         compiler_params=pltpu.CompilerParams(collective_id=1, has_side_effects=True, vmem_limit_bytes=32 << 20),
         name="sublayer",
@@ -470,8 +474,8 @@
         write_kernel,
         out_shape=(pltpu.HBM((TOK, D), BF16), pltpu.HBM((TOK, D), BF16), pltpu.HBM((1, 504), F32), pltpu.HBM((1, 392), F32)),
         in_specs=[vm] * 3,
-        out_specs=(hbm, hbm, pl.BlockSpec(), pl.BlockSpec()),
-        scratch_shapes=[dma((2,))],
+        out_specs=(hbm,) * 4,
+        scratch_shapes=[VMEM((1, 504), F32), VMEM((1, 392), F32), dma((4,))],
         name="write",
     )(*(pltpu.with_memory_space_constraint(v, VMEM) for v in (mixed, grad_hidden, grads)))
     return mixed, grad_hidden, grad_in.reshape(504), grad_out.reshape(392)

time: 70.9 us -> 69.5 us (0.980)
  Pallas kernels: 70.1 us -> 68.7 us
    pallas_call x1, Pallas kernels: 42.7 us -> 41.9 us  [body(): pl.pallas_call(main_kernel, out_shape=(tokens, tokens, sds((1, 1024), F32...]
where the time goes in v5:
time: 69.5 us; the launch traced here: 69.3 us
  Pallas kernels  68.7 us (99%)
    pallas_call x1, Pallas kernels, body(): pl.pallas_call(main_kernel, out_shape=(tokens, tokens, sds((1, 1024), F32...  41.9 us
    pallas_call x1, Pallas kernels, body(): pl.pallas_call(gather_kernel, out_shape=(sds((4, 8, 2, 56, 256), BF16), t...  26 us

profile of v5, /device:TPU:1, one launch (start us, length us, event | category | flops | bytes accessed | tf_op | source)
XLA Modules:
  0.0 69.3 jit_solution(12035341248880591326)
XLA Ops:
  0.6 26.0 %gather.1 = (bf16[4,8,2,56,256]{4,3,2,1,0:T(8,128)(2,1)S(1)}, bf16[128,896]{1,0:T(8,128)(2,1)S(1)}, f32[128,128]{1,0:T(8,128)S(1)}, f32[128,128]{1,0:T(8,128)S(1...) custom-call(bf16[56,576]{1,0:T(8,128)(2,1)} %inc_ref.1, bf16[56,448]{1,0:T(8,128)(2,1)} %bitcast.6, f32[9,28]{1,0:T(8,128)} %bitcast.7, ...), custom_call_target="tpu_custom_call" | custom-call | tf_op jit(solution)/shard_map/gather/pallas_call | solution.py:441
  26.6 41.9 %sublayer.1 = (bf16[128,896]{1,0:T(8,128)(2,1)S(1)}, bf16[128,896]{1,0:T(8,128)(2,1)S(1)}, f32[1,1024]{1,0:T(1,128)S(1)}) custom-call(bf16[4,896,256]{2,1,0:T(8,128)(2,1)S(1)} %bitcast.5, bf16[128,896]{1,0:T(8,128)(2,1)} %hid_hbm.1, bf16[128,896]{1,0:T(8,128)(2,1)} %gm_hbm.1, bf16[128,896]{1,0:T(8,128)(2,1)S(1)} %get-tuple-element.18.nb_ref, ...), custom_call_target="tpu_custom_call" | custom-call | tf_op jit(solution)/shard_map/sublayer/pallas_call | solution.py:454
  68.5 0.8 %write.1 = (bf16[128,896]{1,0:T(8,128)(2,1)}, bf16[128,896]{1,0:T(8,128)(2,1)}, f32[1,504]{1,0:T(1,128)}, f32[1,392]{1,0:T(1,128)}) custom-call(bf16[128,896]{1,0:T(8,128)(2,1)S(1)} %get-tuple-element.23.mixed_ref, bf16[128,896]{1,0:T(8,128)(2,1)S(1)} %get-tuple-element.24.gh_ref, f32[1,1024]{1,0:T(1,128)S(1)} %get-tuple-element.25.grads_ref), custom_call_target="tpu_custom_call" | custom-call | tf_op jit(solution)/shard_map/write/pallas_call | solution.py:473

commit v6 on v5

--- a/solution.py
+++ b/solution.py
@@ -13,6 +13,7 @@
 TOK = 128
 NX, NZ, NY = 4, 16, 8
 NEAR = 2
+FAR_FIRST = (4, 3, 5, 2, 6, 1, 7)
 ROPE_BASE = 1000000.0
 EPS = 1e-06
 VMEM = pltpu.VMEM
@@ -56,7 +57,7 @@
 
 def gather_kernel(
     inc_ref, outc_ref, ins_ref, outs_ref, hid_ref, doc_ref,
-    w_ref, nb_ref, irms_ref, cos_ref, sin_ref, mask_ref,
+    w_ref, nb_ref, nbt_ref, irms_ref, cos_ref, sin_ref, mask_ref,
     ic, oc, ins, outs, hid, doc, pad, lsem, ysend, nsend, yrecv, xsend, xrecv, csend, crecv,
 ):
     x, z, y, c = coords()
@@ -111,7 +112,9 @@
     loads[5].wait()
     rows = hid[...].astype(F32)
     irms = lax.rsqrt(jnp.mean(rows * rows, axis=1, keepdims=True) + EPS)
-    nb_ref[...] = (rows * irms).astype(BF16)
+    normed = rows * irms
+    nb_ref[...] = normed.astype(BF16)
+    nbt_ref[...] = normed.T.astype(BF16)
     irms_ref[...] = jnp.broadcast_to(irms, (TOK, 128))
     mask = jnp.where(allowed_pairs(doc), 1.0, 0.0)
     mask_ref[...] = mask
@@ -155,7 +158,7 @@
 
 
 def main_kernel(
-    w_ref, hid_hbm, gm_hbm, nb_ref, irms_ref, cos_ref, sin_ref, mask_ref,
+    w_ref, hid_hbm, gm_hbm, nb_ref, nbt_ref, irms_ref, cos_ref, sin_ref, mask_ref,
     mixed_ref, gh_ref, gout_ref,
     hid_ref, gm_ref, pin, pout, cin, cout, xin, xout, xrin, xrout, yout, yrout, ybuf, yrbuf, msg, rbuf,
     cs, cr, xs, xr, ys, yr, fs, fr, ls, relay,
@@ -163,8 +166,8 @@
     x, z, y, c = coords()
     me = 2 * y + c
     sib = device(x, z, y, 1 - c)
-    xpeers = [lax.rem(x + k, NX) for k in range(1, NX)]
-    ypeers = [lax.rem(y + k, NY) for k in range(1, NY)]
+    xpeers = [lax.rem(x + k, NX) for k in (2, 1, 3)]
+    ypeers = [lax.rem(y + k, NY) for k in FAR_FIRST]
     group, quad = lax.div(y, 4), lax.rem(y, 4)
     sy, sc = 4 * group + lax.div(lax.rem(z, 8), 2), lax.div(z, 8)
     diagonal = jnp.logical_and(sy == y, sc == c)
@@ -230,8 +233,8 @@
             pout[h, p] = (part[r : r + 32] * grad_scale).astype(BF16)
     pl.semaphore_wait(barrier, 19)
     copies = []
-    for k in range(NY):
-        p = lax.rem(y + 1 + k, NY)
+    for k, step in enumerate(FAR_FIRST + (0,)):
+        p = lax.rem(y + step, NY)
         cp = remote(pout.at[1 - c, p], cout.at[p], cs.at[k], cr.at[p], sib)
         cp.start()
         copies.append(cp)
@@ -272,20 +275,17 @@
         tiles.append((v * cos - swap_halves(v) * sin).astype(BF16))
     tiles.append(jnp.where(lo, gv, zero).astype(BF16))
     gpa = jnp.concatenate(tiles, axis=1)
-    part = lax.dot_general(nb, gpa, TN, preferred_element_type=F32)
-    for h in range(2):
-        for p in range(NX):
-            r = 224 * p + 112 * h
-            pin[h, p] = (part[r : r + 112] * grad_scale).astype(BF16)
-    for k in range(NX):
-        p = lax.rem(x + 1 + k, NX)
-        cp = remote(pin.at[1 - c, p], cin.at[p], cs.at[8 + k], cr.at[8 + p], sib)
+    for p in range(NX):
+        part = jnp.dot(nbt_ref[224 * p : 224 * p + 224], gpa, preferred_element_type=F32)
+        for h in range(2):
+            pin[h, p] = (part[112 * h : 112 * h + 112] * grad_scale).astype(BF16)
+        cp = remote(pin.at[1 - c, p], cin.at[p], cs.at[8 + p], cr.at[8 + p], sib)
         cp.start()
         copies.append(cp)
 
     sum_out = sum_in = None
-    for k in range(NY):
-        p = lax.rem(y + 1 + k, NY)
+    for k, step in enumerate(FAR_FIRST + (0,)):
+        p = lax.rem(y + step, NY)
         remote(pout.at[c, p], cout.at[p], cs.at[0], cr.at[p], sib).wait_recv()
         s = pout[c, p].astype(F32) + cout[p].astype(F32)
         if k < NY - 1:
@@ -438,11 +438,11 @@
     square = sds((TOK, 128), F32)
     held = [pltpu.with_memory_space_constraint(v, pltpu.HBM) for v in (in_codes, out_codes.T, in_scales.T, out_scales, hidden_in, doc_ids)]
     grad_mixed = pltpu.with_memory_space_constraint(grad_mixed, pltpu.HBM)
-    w, nb, irms, cos, sin, mask = pl.pallas_call(
+    w, *rest = pl.pallas_call(
         gather_kernel,
-        out_shape=(sds((4, 8, 2, 56, 256), BF16), tokens, square, square, square, square),
+        out_shape=(sds((4, 8, 2, 56, 256), BF16), tokens, sds((D, TOK), BF16), square, square, square, square),
         in_specs=[hbm] * 6,
-        out_specs=(vm,) * 6,
+        out_specs=(vm,) * 7,
         scratch_shapes=[
             VMEM((56, 576), BF16), VMEM((56, 448), BF16), VMEM((9, 28), F32), VMEM((7, 28), F32),
             VMEM((TOK, D), BF16), VMEM((1, 128), jnp.int32), VMEM((56, 128), F32),
@@ -454,7 +454,7 @@
     mixed, grad_hidden, grads = pl.pallas_call(
         main_kernel,
         out_shape=(tokens, tokens, sds((1, 1024), F32)),
-        in_specs=[vm, hbm, hbm] + [vm] * 5,
+        in_specs=[vm, hbm, hbm] + [vm] * 6,
         out_specs=(vm, vm, vm),
         scratch_shapes=[
             VMEM((TOK, D), BF16), VMEM((TOK, D), BF16),
@@ -469,7 +469,7 @@
         ],
         compiler_params=pltpu.CompilerParams(collective_id=1, has_side_effects=True, vmem_limit_bytes=32 << 20),
         name="sublayer",
-    )(w.reshape(4, D, 256), held[4], grad_mixed, nb, irms, cos, sin, mask)
+    )(w.reshape(4, D, 256), held[4], grad_mixed, *rest)
     mixed, grad_hidden, grad_in, grad_out = pl.pallas_call(
         write_kernel,
         out_shape=(pltpu.HBM((TOK, D), BF16), pltpu.HBM((TOK, D), BF16), pltpu.HBM((1, 504), F32), pltpu.HBM((1, 392), F32)),

time: 69.5 us -> 69 us (level)
  no operation moved by 1% of the time
where the time goes in v6:
time: 69 us; the launch traced here: 68.8 us
  Pallas kernels  68.2 us (99%)
    pallas_call x1, Pallas kernels, body(): pl.pallas_call(main_kernel, out_shape=(tokens, tokens, sds((1, 1024), F32...  41.3 us
    pallas_call x1, Pallas kernels, body(): pl.pallas_call(gather_kernel, out_shape=(sds((4, 8, 2, 56, 256), BF16), t...  26 us

profile of v6, /device:TPU:1, one launch (start us, length us, event | category | flops | bytes accessed | tf_op | source)
XLA Modules:
  0.0 68.8 jit_solution(6669919714182825175)
XLA Ops:
  0.6 26.0 %gather.1 = (bf16[4,8,2,56,256]{4,3,2,1,0:T(8,128)(2,1)S(1)}, bf16[128,896]{1,0:T(8,128)(2,1)S(1)}, bf16[896,128]{1,0:T(8,128)(2,1)S(1)}, f32[128,128]{1,0:T(8,1...) custom-call(bf16[56,576]{1,0:T(8,128)(2,1)} %inc_ref.1, bf16[56,448]{1,0:T(8,128)(2,1)} %bitcast.6, ...), custom_call_target="tpu_custom_call" | custom-call | tf_op jit(solution)/shard_map/gather/pallas_call | solution.py:441
  26.6 41.3 %sublayer.1 = (bf16[128,896]{1,0:T(8,128)(2,1)S(1)}, bf16[128,896]{1,0:T(8,128)(2,1)S(1)}, f32[1,1024]{1,0:T(1,128)S(1)}) custom-call(bf16[4,896,256]{2,1,0:T(8,128)(2,1)S(1)} %bitcast.5, bf16[128,896]{1,0:T(8,128)(2,1)} %hid_hbm.1, bf16[128,896]{1,0:T(8,128)(2,1)} %gm_hbm.1, bf16[128,896]{1,0:T(8,128)(2,1)S(1)} %get-tuple-element.19.nb_ref, ...), custom_call_target="tpu_custom_call" | custom-call | tf_op jit(solution)/shard_map/sublayer/pallas_call | solution.py:454
  68.0 0.8 %write.1 = (bf16[128,896]{1,0:T(8,128)(2,1)}, bf16[128,896]{1,0:T(8,128)(2,1)}, f32[1,504]{1,0:T(1,128)}, f32[1,392]{1,0:T(1,128)}) custom-call(bf16[128,896]{1,0:T(8,128)(2,1)S(1)} %get-tuple-element.25.mixed_ref, bf16[128,896]{1,0:T(8,128)(2,1)S(1)} %get-tuple-element.26.gh_ref, f32[1,1024]{1,0:T(1,128)S(1)} %get-tuple-element.27.grads_ref), custom_call_target="tpu_custom_call" | custom-call | tf_op jit(solution)/shard_map/write/pallas_call | solution.py:473

commit v7 on v6

--- a/solution.py
+++ b/solution.py
@@ -311,17 +311,6 @@
         up = device(x, lax.rem(z + 4 + 8 * k, NZ), y, c)
         pl.semaphore_signal(relay.at[k], inc=1, device_id=up, device_id_type=MESH)
 
-    hid_load.wait()
-    hid = hid_ref[...].astype(F32)
-    out = sum(lax.dot_general(a[:, 256 * t : 256 * t + 256], w_ref[2 + t], NT, preferred_element_type=F32) for t in range(2))
-    mixed_ref[...] = (hid + out).astype(BF16)
-    gn = sum(lax.dot_general(gpa[:, 256 * t : 256 * t + 256], w_ref[t], NT, preferred_element_type=F32) for t in range(2))
-    gn = gn + lax.dot_general(gpa[:, 512:], w_ref[2, :, :128], NT, preferred_element_type=F32)
-    irms = irms_ref[:, :1]
-    normed = hid * irms
-    mean = jnp.mean(gn * normed, axis=1, keepdims=True)
-    gh_ref[...] = ((gn - normed * mean) * irms + gm.astype(F32)).astype(BF16)
-
     row, col = lanes((128, 112), 0), lanes((128, 112))
     from_row = 14 * (2 * ((row >> 4) & 3) + ((row >> 3) & 1)) + 7 * (row >> 6) + (row & 7)
     e_in = jnp.where(((row & 7) < 7) & (col == from_row), 1.0, 0.0).astype(BF16)
@@ -402,6 +391,20 @@
     @pl.when(jnp.logical_not(diagonal))
     def _():
         mine.start()
+
+    hid_load.wait()
+    hid = hid_ref[...].astype(F32)
+    out = sum(lax.dot_general(a[:, 256 * t : 256 * t + 256], w_ref[2 + t], NT, preferred_element_type=F32) for t in range(2))
+    mixed_ref[...] = (hid + out).astype(BF16)
+    gn = sum(lax.dot_general(gpa[:, 256 * t : 256 * t + 256], w_ref[t], NT, preferred_element_type=F32) for t in range(2))
+    gn = gn + lax.dot_general(gpa[:, 512:], w_ref[2, :, :128], NT, preferred_element_type=F32)
+    irms = irms_ref[:, :1]
+    normed = hid * irms
+    mean = jnp.mean(gn * normed, axis=1, keepdims=True)
+    gh_ref[...] = ((gn - normed * mean) * irms + gm.astype(F32)).astype(BF16)
+
+    @pl.when(jnp.logical_not(diagonal))
+    def _():
         mine.wait_send()
         remote(msg.at[0], rbuf.at[z], fs.at[0], fr.at[z], sib).wait_recv()
 

time: 69 us -> 69 us (level)
  no operation moved by 1% of the time
where the time goes in v7:
time: 69 us; the launch traced here: 68.8 us
  Pallas kernels  68.2 us (99%)
    pallas_call x1, Pallas kernels, body(): pl.pallas_call(main_kernel, out_shape=(tokens, tokens, sds((1, 1024), F32...  41.3 us
    pallas_call x1, Pallas kernels, body(): pl.pallas_call(gather_kernel, out_shape=(sds((4, 8, 2, 56, 256), BF16), t...  26 us

profile of v7, /device:TPU:1, one launch (start us, length us, event | category | flops | bytes accessed | tf_op | source)
XLA Modules:
  0.0 68.8 jit_solution(3563042475884266923)
XLA Ops:
  0.6 26.0 %gather.1 = (bf16[4,8,2,56,256]{4,3,2,1,0:T(8,128)(2,1)S(1)}, bf16[128,896]{1,0:T(8,128)(2,1)S(1)}, bf16[896,128]{1,0:T(8,128)(2,1)S(1)}, f32[128,128]{1,0:T(8,1...) custom-call(bf16[56,576]{1,0:T(8,128)(2,1)} %inc_ref.1, bf16[56,448]{1,0:T(8,128)(2,1)} %bitcast.6, ...), custom_call_target="tpu_custom_call" | custom-call | tf_op jit(solution)/shard_map/gather/pallas_call | solution.py:444
  26.6 41.3 %sublayer.1 = (bf16[128,896]{1,0:T(8,128)(2,1)S(1)}, bf16[128,896]{1,0:T(8,128)(2,1)S(1)}, f32[1,1024]{1,0:T(1,128)S(1)}) custom-call(bf16[4,896,256]{2,1,0:T(8,128)(2,1)S(1)} %bitcast.5, bf16[128,896]{1,0:T(8,128)(2,1)} %hid_hbm.1, bf16[128,896]{1,0:T(8,128)(2,1)} %gm_hbm.1, bf16[128,896]{1,0:T(8,128)(2,1)S(1)} %get-tuple-element.19.nb_ref, ...), custom_call_target="tpu_custom_call" | custom-call | tf_op jit(solution)/shard_map/sublayer/pallas_call | solution.py:457
  68.0 0.8 %write.1 = (bf16[128,896]{1,0:T(8,128)(2,1)}, bf16[128,896]{1,0:T(8,128)(2,1)}, f32[1,504]{1,0:T(1,128)}, f32[1,392]{1,0:T(1,128)}) custom-call(bf16[128,896]{1,0:T(8,128)(2,1)S(1)} %get-tuple-element.25.mixed_ref, bf16[128,896]{1,0:T(8,128)(2,1)S(1)} %get-tuple-element.26.gh_ref, f32[1,1024]{1,0:T(1,128)S(1)} %get-tuple-element.27.grads_ref), custom_call_target="tpu_custom_call" | custom-call | tf_op jit(solution)/shard_map/write/pallas_call | solution.py:476
